TPU v7x, 256 devices: a whole 4x4x8 slice. The times are simulated.
256 devices in a mesh: ctx: 32 (over z, x), tp: 8 (over y, core).
Axes of the slice: x: 4, y: 4, z: 8, core: 2. Of those that a mesh axis runs over, the one named last changes fastest.
Arguments:
- embeds: bfloat16 [3, 8, 8192], P(None, None, 'ctx')
- norm_mamba: float32 [8192], P('ctx'), may hold values from 0.1 to 1.9
- in_x: bfloat16 [8192, 16384], P('ctx', 'tp'), may hold values from -0.0625 to 0.0625
- in_z: bfloat16 [8192, 16384], P('ctx', 'tp'), may hold values from -0.0625 to 0.0625
- conv_w: float32 [4, 16384], P(None, 'tp'), may hold values from -3 to 3
- conv_b: float32 [16384], P('tp'), may hold values from -3 to 3
- x_proj: bfloat16 [16384, 544], P('tp'), may hold values from -0.046875 to 0.046875
- dt_norm: float32 [512], replicated, may hold values from 0.1 to 1.9
- b_norm: float32 [16], replicated, may hold values from 0.1 to 1.9
- c_norm: float32 [16], replicated, may hold values from 0.1 to 1.9
- dt_proj: bfloat16 [512, 16384], P(None, 'tp'), may hold values from -0.25 to 0.25
- dt_bias: float32 [16384], P('tp'), may hold values from -3 to 0
- a_log: float32 [16, 16384], P(None, 'tp'), may hold values from 0 to 2.77
- d_skip: float32 [16384], P('tp'), may hold values from 0.5 to 1.5
- out_proj: bfloat16 [16384, 8192], P('tp', 'ctx'), may hold values from -0.046875 to 0.046875
- norm_attn: float32 [8192], P('ctx'), may hold values from 0.1 to 1.9
- w_query: bfloat16 [8192, 8192], P('ctx', 'tp'), may hold values from -0.0625 to 0.0625
- key_matrix: bfloat16 [8192, 1024], P('ctx', 'tp'), may hold values from -0.0625 to 0.0625
- value_matrix: bfloat16 [8192, 1024], P('ctx', 'tp'), may hold values from -0.0625 to 0.0625
- w_out: bfloat16 [8192, 8192], P('tp', 'ctx'), may hold values from -0.0625 to 0.0625
- cache_k: bfloat16 [8, 16384, 1024], P(None, 'ctx', 'tp')
- value_cache: bfloat16 [8, 16384, 1024], P(None, 'ctx', 'tp'), may hold values from -6 to 6
- lengths: int32 [8], replicated, may hold values from 1 to 16384, as said below
- block_of_slot: int32 [8, 128], P(None, 'ctx'), may hold values from 0 to 127, as said below
- conv_state: float32 [8, 3, 16384], P(None, None, 'tp'), may hold values from -6 to 6
- ssm_state: float32 [8, 16, 16384], P(None, None, 'tp'), may hold values from -6 to 6
Outputs:
- hidden_out: float32 [3, 8, 8192], P(None, None, 'ctx')
- new_keys: bfloat16 [3, 8, 1024], P(None, None, 'tp')
- new_values: bfloat16 [3, 8, 1024], P(None, None, 'tp')
- ssm_out: float32 [8, 16, 16384], P(None, None, 'tp')
- conv_out: float32 [8, 3, 16384], P(None, None, 'tp')
Inputs may be any that keep to these rules, and one draw needn't show every extreme that they name: Each row of block_of_slot is a permutation of 0 .. 127. `lengths`: some row has all 16384 slots filled.
All inputs are finite; a program needn't handle non-finite values.
Results may differ from a plain program's by a relative error of at most 0.025.
Values may be sent and summed in bfloat16 or wider, within the bound.
No kernel may reach another device: no remote copies, remote signals or barrier semaphores. Data moves between devices by JAX's collectives and lax.ppermute only.
A program may use at most 128 MiB of HBM per device.

v0:
```python
import functools

import jax
import jax.numpy as jnp
from jax import lax
from jax.experimental import pallas as pl
from jax.experimental.pallas import tpu as pltpu
from jax.sharding import Mesh, PartitionSpec as P

DS = 16
DTR = 512
HEAD = 128
BLK = 128
STEPS = 3
ROWS = 8
ALL_ROWS = STEPS * ROWS
LANES = 128
X_SIZE = 4
CTX = ("za", "zb", "x")
TP = ("y", "core")
FLOPS = 3_000_000_000
GROUPS = 4
NEGATIVE = -1e30
bf16 = jnp.bfloat16
f32 = jnp.float32


def exchange(parts, axis):
    return lax.all_to_all(parts, axis, 0, 0, tiled=True)


def from_partners(part, axis="x"):
    received = {
        flip: lax.ppermute(part, axis, [(i, i ^ flip) for i in range(4)]) for flip in (1, 3, 2)
    }
    return received[1], received[2], received[3]


def from_other(part, axis):
    return lax.ppermute(part, axis, [(0, 1), (1, 0)])


def over_cores(part):
    return part + from_other(part, "core")


def call(kernel, outs, *operands, vmem_mib=48, **options):
    return pl.pallas_call(
        kernel,
        out_shape=[jax.ShapeDtypeStruct(shape, dtype) for shape, dtype in outs],
        compiler_params=pltpu.CompilerParams(vmem_limit_bytes=vmem_mib * 1024 * 1024),
        cost_estimate=pl.CostEstimate(flops=FLOPS, bytes_accessed=8 << 20, transcendentals=0),
        **options,
    )(*operands)


def lane_index(rows, lanes=LANES):
    return lax.broadcasted_iota(jnp.int32, (rows, lanes), 1)


def row_index(rows, lanes=LANES):
    return lax.broadcasted_iota(jnp.int32, (rows, lanes), 0)


def rounded(value):
    return value.astype(bf16).astype(f32)


def silu(value):
    return value / (1.0 + jnp.exp(-value))


def project_kernel(
    rows_hbm, gain_hbm, wx_hbm, wz_hbm, out_ref, rows_ref, gain_ref, wx_ref, wz_ref, sems, small_sems
):
    small = [
        pltpu.make_async_copy(rows_hbm, rows_ref, small_sems.at[0]),
        pltpu.make_async_copy(gain_hbm, gain_ref, small_sems.at[1]),
    ]
    for copy in small:
        copy.start()
    copies = []
    for half, (source, target) in enumerate(((wx_hbm, wx_ref), (wz_hbm, wz_ref))):
        copies.append(pltpu.make_async_copy(source, target, sems.at[half]))
        copies[-1].start()
    for copy in small:
        copy.wait()
    rows = rows_ref[...].astype(f32)
    scaled = (rows * gain_ref[...]).astype(bf16)
    column = jnp.sum(rows * rows, axis=1, keepdims=True)
    eye = row_index(ALL_ROWS) == lane_index(ALL_ROWS)
    squares = jnp.sum(jnp.where(eye, column, 0.0), axis=0, keepdims=True)
    hi = rounded(squares)
    which = row_index(8)
    stats = jnp.where(which == 0, hi, jnp.where(which == 1, squares - hi, 0.0))
    for half, weight_ref in enumerate((wx_ref, wz_ref)):
        copies[half].wait()
        part = jnp.dot(scaled, weight_ref[...], preferred_element_type=f32)
        for k in range(out_ref.shape[1]):
            chunk = part[:, k * LANES : (k + 1) * LANES]
            out_ref[half, k] = jnp.concatenate([chunk, stats], axis=0).astype(bf16)


def reduce_kernel(width_all, in_ref, out_ref):
    total = in_ref[0].astype(f32)
    for source in range(1, in_ref.shape[0]):
        total = total + in_ref[source].astype(f32)
    squares = total[ALL_ROWS : ALL_ROWS + 1] + total[ALL_ROWS + 1 : ALL_ROWS + 2]
    eye = row_index(ALL_ROWS) == lane_index(ALL_ROWS)
    column = jnp.sum(jnp.where(eye, squares, 0.0), axis=1, keepdims=True)
    mine = (total[:ALL_ROWS] * lax.rsqrt(column / width_all + 1e-06)).astype(bf16)
    for target in range(out_ref.shape[0]):
        out_ref[target] = mine


def conv_kernel(inner_ref, hist_ref, taps_ref, bias_ref, xp_ref, low_ref, mixed_ref, hist_out_ref, mixed16):
    for k in range(mixed_ref.shape[1] // LANES):
        cols = slice(k * LANES, (k + 1) * LANES)
        fresh = inner_ref[k].astype(f32)
        window = [hist_ref[t, :, cols] for t in range(STEPS)]
        window += [fresh[s * ROWS : (s + 1) * ROWS] for s in range(STEPS)]
        taps = taps_ref[:, cols]
        bias = bias_ref[:, cols]
        mixed = []
        for s in range(STEPS):
            total = window[s] * taps[0:1]
            for t in range(1, STEPS + 1):
                total = total + window[s + t] * taps[t : t + 1]
            mixed.append(silu(total + bias))
            hist_out_ref[s, :, cols] = window[STEPS + s]
        mixed = jnp.concatenate(mixed, axis=0)
        mixed_ref[:, cols] = mixed
        mixed16[:, cols] = mixed.astype(bf16)
    low = lax.dot_general(
        mixed16[...], xp_ref[...], (((1,), (1,)), ((), ())), preferred_element_type=f32
    ).astype(bf16)
    low_ref[...] = low


def scan_kernel(
    own_ref, one_ref, two_ref, three_ref, dt_gain_ref, b_gain_ref, c_gain_ref, dt_bias_ref, a_ref, skip_ref, mixed_ref, gate_ref,
    state_hbm, dtp_hbm, op_hbm, state_out_hbm, part_ref,
    dtp_ref, op_ref, state_ref, b_wide, c_wide, decay_wide, sems, state_sems,
):
    tiles = state_ref.shape[0]
    group = tiles // GROUPS
    dtp_copy = pltpu.make_async_copy(dtp_hbm, dtp_ref, sems.at[0])
    op_copy = pltpu.make_async_copy(op_hbm, op_ref, sems.at[1])
    dtp_copy.start()
    entering, leaving = [], []
    for i in range(GROUPS):
        at = pl.ds(i * group, group)
        entering.append(
            pltpu.make_async_copy(state_hbm.at[at], state_ref.at[at], state_sems.at[0, i])
        )
        entering[i].start()
        leaving.append(
            pltpu.make_async_copy(state_ref.at[at], state_out_hbm.at[at], state_sems.at[1, i])
        )
    op_copy.start()
    low = sum_refs((own_ref, one_ref, two_ref, three_ref))
    raw = low[:, :DTR]
    mean_sq = jnp.sum(raw * raw, axis=1, keepdims=True) / DTR
    dt_low = (raw * lax.rsqrt(mean_sq + 1e-06) * dt_gain_ref[...]).astype(bf16)
    for wide, gain_ref, at in ((b_wide, b_gain_ref, DTR), (c_wide, c_gain_ref, DTR + DS)):
        raw = low[:, at : at + DS]
        mean_sq = jnp.sum(raw * raw, axis=1, keepdims=True) / DS
        normed = raw * lax.rsqrt(mean_sq + 1e-06) * gain_ref[...]
        for n in range(DS):
            wide[n] = jnp.broadcast_to(normed[:, n : n + 1], (ALL_ROWS, LANES))
    for tile in range(tiles):
        decay = -jnp.exp(a_ref[:, tile * LANES : (tile + 1) * LANES])
        for n in range(DS):
            decay_wide[tile, n] = jnp.broadcast_to(decay[n : n + 1], (ROWS, LANES))
    dtp_copy.wait()
    raw = jnp.dot(dt_low, dtp_ref[...], preferred_element_type=f32) + dt_bias_ref[...]
    steps = jnp.maximum(raw, 0.0) + jnp.log1p(jnp.exp(-jnp.abs(raw)))
    mixed = mixed_ref[...]
    drive = steps * mixed
    scanned = []
    for tile in range(tiles):
        cols = slice(tile * LANES, (tile + 1) * LANES)
        if tile % group == 0:
            entering[tile // group].wait()
        y = [jnp.zeros((ROWS, LANES), f32) for _ in range(STEPS)]
        for n in range(DS):
            state = state_ref[tile, n]
            decay = decay_wide[tile, n]
            for s in range(STEPS):
                rows = slice(s * ROWS, (s + 1) * ROWS)
                state = (
                    jnp.exp(steps[rows, cols] * decay) * state + drive[rows, cols] * b_wide[n, rows]
                )
                y[s] = y[s] + c_wide[n, rows] * state
            state_ref[tile, n] = state
        if tile % group == group - 1:
            leaving[tile // group].start()
        y = jnp.concatenate(y, axis=0) + skip_ref[:, cols] * mixed[:, cols]
        scanned.append((y * silu(gate_ref[tiles + tile].astype(f32))).astype(bf16))
    op_copy.wait()
    total = jnp.dot(jnp.concatenate(scanned, axis=1), op_ref[...], preferred_element_type=f32)
    part = total.astype(bf16)
    for target in range(part_ref.shape[0]):
        part_ref[target] = part
    for copy in leaving:
        copy.wait()


def qkv_kernel(parts_ref, rows_ref, gain_ref, wq_ref, wk_ref, wv_ref, residual_ref, out_ref):
    total = parts_ref[0].astype(f32)
    for source in range(1, parts_ref.shape[0]):
        total = total + parts_ref[source].astype(f32)
    residual = rows_ref[...].astype(f32) + total
    residual_ref[...] = residual
    scaled = (residual * gain_ref[...]).astype(bf16)
    column = jnp.sum(residual * residual, axis=1, keepdims=True)
    at = 0
    for weight_ref in (wq_ref, wk_ref, wv_ref):
        width = weight_ref.shape[1]
        out_ref[:, at : at + width] = jnp.dot(
            scaled, weight_ref[...], preferred_element_type=f32
        ).astype(bf16)
        at += width
    out_ref[:, at:] = pair_columns(column).astype(bf16)


def pair_columns(column):
    hi = rounded(column)
    which = lane_index(ALL_ROWS)
    return jnp.where(which == 0, hi, jnp.where(which == 1, column - hi, 0.0))


def sum_refs(refs):
    parts = [ref[...].astype(f32) for ref in refs]
    if len(parts) == 2:
        return parts[0] + parts[1]
    return (parts[0] + parts[1]) + (parts[2] + parts[3])


def qkv_sum_kernel(*refs):
    out_ref = refs[-1]
    total = sum_refs(refs[:-1])
    column = jnp.sum(total[:, -LANES:], axis=1, keepdims=True)
    out_ref[:, :-LANES] = total[:, :-LANES].astype(bf16)
    out_ref[:, -LANES:] = pair_columns(column).astype(bf16)


def pack_logs(logs):
    which = lane_index(ALL_ROWS)
    logs = jnp.where(which < ROWS, logs, 0.0)
    hi = rounded(logs)
    mid = rounded(logs - hi)
    low = logs - hi - mid
    return hi + pltpu.roll(mid, ROWS, 1) + pltpu.roll(low, 2 * ROWS, 1)


def unpack_logs(packed):
    return (
        packed + pltpu.roll(packed, LANES - ROWS, 1) + pltpu.roll(packed, LANES - 2 * ROWS, 1)
    )


def attention_kernel(
    width_all, first_ref, lengths_ref, blocks_ref, own_ref, one_ref, two_ref, three_ref,
    keys_ref, values_ref,
    new_keys_ref, new_values_ref, out_ref, query, fresh_k, fresh_v,
):
    total = sum_refs((own_ref, one_ref, two_ref, three_ref))
    column = jnp.sum(total[:, -LANES:], axis=1, keepdims=True)
    total = rounded(total[:, :-LANES] * lax.rsqrt(column / width_all + 1e-06))
    heads = total.shape[1] // HEAD - 2
    queries = STEPS * heads
    keys_now = total[:, heads * HEAD : (heads + 1) * HEAD]
    values_now = total[:, (heads + 1) * HEAD :]
    new_keys_ref[...] = keys_now.astype(bf16)
    new_values_ref[...] = values_now.astype(bf16)
    fresh_k[...] = jnp.zeros_like(fresh_k)
    fresh_v[...] = jnp.zeros_like(fresh_v)
    for s in range(STEPS):
        rows = slice(s * ROWS, (s + 1) * ROWS)
        fresh_k[pl.ds(s, ROWS, stride=8), :] = keys_now[rows]
        fresh_v[pl.ds(s, ROWS, stride=8), :] = values_now[rows]
        for g in range(heads):
            query[pl.ds(s * heads + g, ROWS, stride=queries), :] = total[
                rows, g * HEAD : (g + 1) * HEAD
            ]
    which = lane_index(queries, 8)
    fresh_live = (which * heads <= row_index(queries, 8)) & (which < STEPS)
    fresh_live = fresh_live & (first_ref[0] == 1)
    score_scale = HEAD**-0.5
    lanes = lane_index(queries)
    contract = (((1,), (1,)), ((), ()))
    every = range(ROWS)
    scores, fresh, live = [], [], []
    for b in every:
        query_b = query[b * queries : (b + 1) * queries, :].astype(bf16)
        scores.append(
            lax.dot_general(query_b, keys_ref[b], contract, preferred_element_type=f32)
        )
        fresh.append(
            lax.dot_general(
                query_b,
                fresh_k[b * 8 : (b + 1) * 8, :].astype(bf16),
                contract,
                preferred_element_type=f32,
            )
        )
        live.append(
            jnp.concatenate(
                [
                    lanes < lengths_ref[b] - blocks_ref[k, b] * BLK
                    for k in range(keys_ref.shape[1] // BLK)
                ],
                axis=1,
            )
        )
    scores = [jnp.where(live[b], scores[b] * score_scale, NEGATIVE) for b in every]
    fresh = [jnp.where(fresh_live, fresh[b] * score_scale, NEGATIVE) for b in every]
    peaks = [
        jnp.maximum(
            jnp.max(scores[b], axis=1, keepdims=True), jnp.max(fresh[b], axis=1, keepdims=True)
        )
        for b in every
    ]
    weights = [jnp.where(live[b], jnp.exp(scores[b] - peaks[b]), 0.0) for b in every]
    fresh = [jnp.where(fresh_live, jnp.exp(fresh[b] - peaks[b]), 0.0) for b in every]
    attended = [
        jnp.dot(weights[b].astype(bf16), values_ref[b], preferred_element_type=f32)
        + jnp.dot(
            fresh[b].astype(bf16),
            fresh_v[b * 8 : (b + 1) * 8, :].astype(bf16),
            preferred_element_type=f32,
        )
        for b in every
    ]
    sums = [
        jnp.sum(weights[b], axis=1, keepdims=True) + jnp.sum(fresh[b], axis=1, keepdims=True)
        for b in every
    ]
    logs = jnp.zeros((queries, LANES), f32)
    for b in every:
        any_live = sums[b] > 0
        safe = jnp.where(any_live, sums[b], 1.0)
        out_ref[b] = (attended[b] / safe).astype(bf16)
        log_sum = jnp.where(any_live, peaks[b] + jnp.log(safe), NEGATIVE)
        logs = jnp.where(lanes == b, log_sum, logs)
    out_ref[ROWS] = pack_logs(logs).astype(bf16)


def shares_of(refs):
    logs = [unpack_logs(ref[ROWS].astype(f32)) for ref in refs]
    top = functools.reduce(jnp.maximum, logs)
    shares = [jnp.exp(log - top) for log in logs]
    total = functools.reduce(jnp.add, shares)
    return [share / total for share in shares], top + jnp.log(total)


def combined_row(refs, shares, b):
    attended = [shares[i][:, b : b + 1] * ref[b].astype(f32) for i, ref in enumerate(refs)]
    return functools.reduce(jnp.add, attended)


def combine_kernel(*refs):
    refs, out_ref = refs[:-1], refs[-1]
    shares, logs = shares_of(refs)
    for b in range(ROWS):
        out_ref[b] = combined_row(refs, shares, b).astype(bf16)
    out_ref[ROWS] = pack_logs(logs).astype(bf16)


def finish_kernel(own_ref, one_ref, two_ref, three_ref, weight_ref, out_ref, attended):
    refs = (own_ref, one_ref, two_ref, three_ref)
    shares, _ = shares_of(refs)
    for b in range(ROWS):
        queries = shares[0].shape[0]
        attended[b * queries : (b + 1) * queries, :] = combined_row(refs, shares, b)
    heads = queries // STEPS
    rows = jnp.concatenate(
        [
            jnp.concatenate(
                [
                    attended[pl.ds(s * heads + g, ROWS, stride=queries), :]
                    for g in range(heads)
                ],
                axis=1,
            )
            for s in range(STEPS)
        ],
        axis=0,
    ).astype(bf16)
    part = jnp.dot(rows, weight_ref[...], preferred_element_type=f32).astype(bf16)
    out_ref[...] = part


def body(
    embeds, norm_mamba, in_x, in_z, conv_w, conv_b, x_proj, dt_norm, b_norm, c_norm, dt_proj,
    dt_bias, a_log, d_skip, out_proj, norm_attn, w_query, key_matrix, value_matrix, w_out,
    cache_k, value_cache, lengths, block_of_slot, conv_state, ssm_state,
):
    ctx_size, tp_size = (lax.axis_size(axis) for axis in (CTX, TP))
    local_width = embeds.shape[2]
    width_all = float(local_width * ctx_size)
    channels = in_x.shape[1]
    heads = w_query.shape[1] // HEAD
    queries = STEPS * heads
    chunk_count = channels // LANES
    rows_in = embeds.reshape(ALL_ROWS, local_width)

    hbm = pl.BlockSpec(memory_space=pltpu.HBM)
    vmem = pl.BlockSpec(memory_space=pltpu.VMEM)
    (chunks,) = call(
        project_kernel,
        [((2, chunk_count, 32, LANES), bf16)],
        rows_in,
        norm_mamba.reshape(1, -1),
        in_x,
        in_z,
        vmem_mib=62,
        in_specs=[hbm] * 4,
        scratch_shapes=[
            pltpu.VMEM((ALL_ROWS, local_width), bf16),
            pltpu.VMEM((1, local_width), f32),
            pltpu.VMEM(in_x.shape, bf16),
            pltpu.VMEM(in_z.shape, bf16),
            pltpu.SemaphoreType.DMA((2,)),
            pltpu.SemaphoreType.DMA((2,)),
        ],
    )
    received = exchange(chunks.reshape(2 * chunk_count, 32, LANES), CTX)
    (mine,) = call(
        functools.partial(reduce_kernel, width_all),
        [((ctx_size, ALL_ROWS, LANES), bf16)],
        received,
    )
    inner = exchange(mine, CTX)

    low, mixed, history = call(
        conv_kernel,
        [
            ((ALL_ROWS, DTR + 2 * DS), bf16),
            ((ALL_ROWS, channels), f32),
            ((STEPS, ROWS, channels), f32),
        ],
        inner,
        conv_state.transpose(1, 0, 2),
        conv_w,
        conv_b.reshape(1, -1),
        x_proj.T,
        scratch_shapes=[pltpu.VMEM((ALL_ROWS, channels), bf16)],
    )
    low = over_cores(low)
    tiled = (chunk_count, DS, ROWS, LANES)
    state = ssm_state.reshape(ROWS, DS, chunk_count, LANES).transpose(2, 1, 0, 3)
    state, part = call(
        scan_kernel,
        [(tiled, f32), ((tp_size, ALL_ROWS, local_width), bf16)],
        low,
        *from_partners(low, "y"),
        dt_norm.reshape(1, -1),
        b_norm.reshape(1, -1),
        c_norm.reshape(1, -1),
        dt_bias.reshape(1, -1),
        a_log,
        d_skip.reshape(1, -1),
        mixed,
        inner,
        state,
        dt_proj,
        out_proj,
        vmem_mib=53,
        in_specs=[vmem] * 12 + [hbm] * 3,
        out_specs=[hbm, vmem],
        scratch_shapes=[
            pltpu.VMEM(dt_proj.shape, bf16),
            pltpu.VMEM(out_proj.shape, bf16),
            pltpu.VMEM(tiled, f32),
            pltpu.VMEM((DS, ALL_ROWS, LANES), f32),
            pltpu.VMEM((DS, ALL_ROWS, LANES), f32),
            pltpu.VMEM(tiled, f32),
            pltpu.SemaphoreType.DMA((2,)),
            pltpu.SemaphoreType.DMA((2, GROUPS)),
        ],
    )
    state = state.transpose(2, 1, 0, 3).reshape(ssm_state.shape)
    part = exchange(part, TP)

    packed_width = (heads + 3) * HEAD
    residual, projected = call(
        qkv_kernel,
        [((ALL_ROWS, local_width), f32), ((ALL_ROWS, packed_width), bf16)],
        part,
        rows_in,
        norm_attn.reshape(1, -1),
        w_query,
        key_matrix,
        value_matrix,
    )
    shape = ((ALL_ROWS, packed_width), bf16)
    (projected,) = call(qkv_sum_kernel, [shape], projected, *from_partners(projected))
    (projected,) = call(qkv_sum_kernel, [shape], projected, from_other(projected, "zb"))
    others = from_partners(projected, "za")
    *others, state = lax.optimization_barrier((*others, state))

    first = (lax.axis_index(CTX) == 0).astype(jnp.int32).reshape(1)
    new_keys, new_values, attended = call(
        functools.partial(attention_kernel, width_all),
        [
            ((ALL_ROWS, HEAD), bf16),
            ((ALL_ROWS, HEAD), bf16),
            ((ROWS + 1, queries, HEAD), bf16),
        ],
        first,
        lengths,
        block_of_slot.T,
        projected,
        *others,
        cache_k,
        value_cache,
        in_specs=[pl.BlockSpec(memory_space=pltpu.SMEM)] * 3 + [vmem] * 6,
        scratch_shapes=[
            pltpu.VMEM((ROWS * queries, HEAD), f32),
            pltpu.VMEM((ROWS * 8, HEAD), f32),
            pltpu.VMEM((ROWS * 8, HEAD), f32),
        ],
    )
    shape = (attended.shape, bf16)
    (attended,) = call(combine_kernel, [shape], attended, *from_partners(attended))
    (attended,) = call(combine_kernel, [shape], attended, from_other(attended, "zb"))
    (part,) = call(
        finish_kernel,
        [((ALL_ROWS, local_width), bf16)],
        attended,
        *from_partners(attended, "za"),
        w_out,
        scratch_shapes=[pltpu.VMEM((ROWS * queries, HEAD), f32)],
    )
    part = over_cores(part)
    one, two, three = (other.astype(f32) for other in from_partners(part, "y"))
    hidden = residual + ((part.astype(f32) + one) + (two + three))
    return (
        hidden.reshape(STEPS, ROWS, local_width),
        new_keys.reshape(STEPS, ROWS, HEAD),
        new_values.reshape(STEPS, ROWS, HEAD),
        state,
        history.transpose(1, 0, 2),
    )


def solution(mesh):
    ctx_size, tp_size = mesh.devices.shape
    split = Mesh(
        mesh.devices.reshape(ctx_size // X_SIZE // 2, 2, X_SIZE, tp_size // 2, 2),
        ("za", "zb", "x", "y", "core"),
    )
    return jax.shard_map(
        body,
        mesh=split,
        in_specs=(
            P(None, None, CTX),
            P(CTX),
            P(CTX, TP),
            P(CTX, TP),
            P(None, TP),
            P(TP),
            P(TP, None),
            P(),
            P(),
            P(),
            P(None, TP),
            P(TP),
            P(None, TP),
            P(TP),
            P(TP, CTX),
            P(CTX),
            P(CTX, TP),
            P(CTX, TP),
            P(CTX, TP),
            P(TP, CTX),
            P(None, CTX, TP),
            P(None, CTX, TP),
            P(),
            P(None, CTX),
            P(None, None, TP),
            P(None, None, TP),
        ),
        out_specs=(
            P(None, None, CTX),
            P(None, None, TP),
            P(None, None, TP),
            P(None, None, TP),
            P(None, None, TP),
        ),
        check_vma=False,
    )
```

profile of v0, /device:TPU:6, one launch (start us, length us, event | category | flops | bytes accessed | tf_op | source)
XLA Modules:
  0.0 126.8 jit_solution(15002725524137488993)
XLA Ops:
  0.6 2.6 %shard_map.281 = bf16[2,16,32,128]{3,2,1,0:T(8,128)(2,1)} custom-call(bf16[24,256]{1,0:T(8,128)(2,1)} %bitcast.31, f32[1,256]{1,0:T(1,128)} %bitcast.46, bf16[256,2048]{1,0:T(8,128)(2,1)} %wx_hbm.1, bf16[256,2048]{1,0:T(8,128)(2,1)} %wz_hbm.1), custom_call_target="tpu_custom_call" | custom-call | flops 3000000000 | bytes 8388608 | tf_op jit(solution)/shard_map/pallas_call | solution.py:48
  3.2 22.8 %all_to_all.15.in_ref = bf16[32,32,128]{2,1,0:T(8,128)(2,1)S(1)} all-to-all(bf16[32,32,128]{2,1,0:T(8,128)(2,1)} %bitcast.45), channel_id=1, replica_groups=mesh['za'=4,'zb'=2,'x'=4,'y'=4,'core'=2] {'za','zb','x'}, dimensions={0} | all-to-all | bytes 524288 | tf_op jit(solution)/shard_map/all_to_all | solution.py:29
  26.2 14.9 %all_to_all.16.inner_ref.gate_ref = bf16[32,24,128]{2,1,0:T(8,128)(2,1)S(1)} all-to-all(bf16[32,24,128]{2,1,0:T(8,128)(2,1)S(1)} %shard_map.282), channel_id=1, replica_groups=mesh['za'=4,'zb'=2,'x'=4,'y'=4,'core'=2] {'za','zb','x'}, dimensions={0} | all-to-all | bytes 393216 | tf_op jit(solution)/shard_map/all_to_all | solution.py:29
  41.1 1.3 %shard_map.283 = (bf16[24,544]{1,0:T(8,128)(2,1)S(1)}, f32[24,2048]{1,0:T(8,128)S(1)}, f32[3,8,2048]{2,1,0:T(8,128)}) custom-call(bf16[32,24,128]{2,1,0:T(8,128)(2,1)S(1)} %all_to_all.16.inner_ref.gate_ref, f32[3,8,2048]{2,1,0:T(8,128)S(1)} %bitcast.30, f32[4,2048]{1,0:T(4,128)S(1)} %copy-done.9, f32[1,2048]{1,0:T(1,128)S(1)} %bitcast.33, ...), custom_call_target="tpu_custom_call" | custom-call | flops 3000000000 | bytes 8388608 | tf_op jit(solution)/shard_map/pallas_call | solution.py:48
  42.6 1.2 collective-permute-done
  43.8 1.7 %collective-permute-start.1 = (bf16[24,544]{1,0:T(8,128)(2,1)S(1)}, bf16[24,544]{1,0:T(8,128)(2,1)S(1)}, u32[]{:S(2)}, u32[]{:S(2)}) collective-permute-start(bf16[24,544]{1,0:T(8,128)(2,1)S(1)} %add.24.own_ref), channel_id=1, source_target_pairs={{0,2},{2,0},{4,6},{6,4},{1,3},{3,1},{5,7},{7,5},{8,10},{10,8},{12,... | collective-permute-start | bytes 78344 | tf_op jit(solution)/shard_map/ppermute | solution.py:34
  45.5 2.9 %collective-permute-start.2 = (bf16[24,544]{1,0:T(8,128)(2,1)S(1)}, bf16[24,544]{1,0:T(8,128)(2,1)S(1)}, u32[]{:S(2)}, u32[]{:S(2)}) collective-permute-start(bf16[24,544]{1,0:T(8,128)(2,1)S(1)} %add.24.own_ref), channel_id=1, source_target_pairs={{0,4},{2,6},{4,0},{6,2},{1,5},{3,7},{5,1},{7,3},{8,12},{10,14},{12... | collective-permute-start | bytes 78344 | tf_op jit(solution)/shard_map/ppermute | solution.py:34
  48.8 1.6 %copy.35 = f32[8,16,16,128]{3,0,1,2:T(8,128)} copy(f32[8,16,16,128]{3,2,1,0:T(8,128)S(1)} %bitcast.41) | data formatting | bytes 2097152 | tf_op jit(solution)/shard_map/reshape | solution.py:453
  50.9 2.6 %collective-permute-done.3.three_ref = bf16[24,544]{1,0:T(8,128)(2,1)S(1)} collective-permute-done((bf16[24,544]{1,0:T(8,128)(2,1)S(1)}, bf16[24,544]{1,0:T(8,128)(2,1)S(1)}, u32[]{:S(2)}, u32[]{:S(2)}) %collective-permute-start.3) | collective-permute-done | bytes 26144 | tf_op jit(solution)/shard_map/ppermute | solution.py:34
  53.6 4.1 %shard_map.284 = (f32[16,16,8,128]{3,2,1,0:T(8,128)}, bf16[8,24,256]{2,1,0:T(8,128)(2,1)S(1)}) custom-call(bf16[24,544]{1,0:T(8,128)(2,1)S(1)} %add.24.own_ref, bf16[24,544]{1,0:T(8,128)(2,1)S(1)} %collective-permute-done.1.one_ref, bf16[24,544]{1,0:T(8,128)(2,1)S(1)} %collective-permute-done.2.two_ref, ...), custom_call_target="tpu_custom_call" | custom-call | flops 3000000000 | bytes 8388608 | tf_op jit(solution)/shard_map/pallas_call | solution.py:48
  57.7 8.2 %all_to_all.17.parts_ref = bf16[8,24,256]{2,1,0:T(8,128)(2,1)S(1)} all-to-all(bf16[8,24,256]{2,1,0:T(8,128)(2,1)S(1)} %get-tuple-element.21), channel_id=1, replica_groups=mesh['za'=4,'zb'=2,'x'=4,'y'=4,'core'=2] {'y','core'}, dimensions={0} | all-to-all | bytes 196608 | tf_op jit(solution)/shard_map/all_to_all | solution.py:29
  66.7 3.0 %collective-permute-start.5 = (bf16[24,1408]{1,0:T(8,128)(2,1)S(1)}, bf16[24,1408]{1,0:T(8,128)(2,1)S(1)}, u32[]{:S(2)}, u32[]{:S(2)}) collective-permute-start(bf16[24,1408]{1,0:T(8,128)(2,1)S(1)} %get-tuple-element.23.refs_0_), channel_id=1, source_target_pairs={{0,16},{8,24},{16,0},{24,8},{1,17},{9,25},{17,1},{25,9},{2,18},{10... | collective-permute-start | bytes 202760 | tf_op jit(solution)/shard_map/ppermute | solution.py:34
  69.7 1.2 collective-permute-start.6
  70.9 2.0 %collective-permute-done.5.refs_2_ = bf16[24,1408]{1,0:T(8,128)(2,1)S(1)} collective-permute-done((bf16[24,1408]{1,0:T(8,128)(2,1)S(1)}, bf16[24,1408]{1,0:T(8,128)(2,1)S(1)}, u32[]{:S(2)}, u32[]{:S(2)}) %collective-permute-start.5) | collective-permute-done | bytes 67616 | tf_op jit(solution)/shard_map/ppermute | solution.py:34
  72.9 2.3 %collective-permute-done.6.refs_3_ = bf16[24,1408]{1,0:T(8,128)(2,1)S(1)} collective-permute-done((bf16[24,1408]{1,0:T(8,128)(2,1)S(1)}, bf16[24,1408]{1,0:T(8,128)(2,1)S(1)}, u32[]{:S(2)}, u32[]{:S(2)}) %collective-permute-start.6) | collective-permute-done | bytes 67616 | tf_op jit(solution)/shard_map/ppermute | solution.py:34
  76.0 3.9 %collective-permute-done.7.refs_1_ = bf16[24,1408]{1,0:T(8,128)(2,1)S(1)} collective-permute-done((bf16[24,1408]{1,0:T(8,128)(2,1)S(1)}, bf16[24,1408]{1,0:T(8,128)(2,1)S(1)}, u32[]{:S(2)}, u32[]{:S(2)}) %collective-permute-start.7) | collective-permute-done | bytes 67616 | tf_op jit(solution)/shard_map/ppermute | solution.py:40
  81.4 5.3 %collective-permute-start.9 = (bf16[24,1408]{1,0:T(8,128)(2,1)S(1)}, bf16[24,1408]{1,0:T(8,128)(2,1)S(1)}, u32[]{:S(2)}, u32[]{:S(2)}) collective-permute-start(bf16[24,1408]{1,0:T(8,128)(2,1)S(1)} %shard_map.287.own_ref), channel_id=1, source_target_pairs={{0,128},{64,192},{128,0},{192,64},{1,129},{65,193},{129,1},{193,65... | collective-permute-start | bytes 202760 | tf_op jit(solution)/shard_map/ppermute | solution.py:34
  86.7 1.8 %copy.32 = f32[8,16,16,128]{3,2,1,0:T(8,128)S(1)} copy(f32[8,16,16,128]{3,0,1,2:T(8,128)} %bitcast.43) | data formatting | bytes 2097152 | tf_op jit(solution)/shard_map/transpose | solution.py:484
  89.8 1.9 %shard_map.288 = (bf16[24,128]{1,0:T(8,128)(2,1)}, bf16[24,128]{1,0:T(8,128)(2,1)}, bf16[9,24,128]{2,1,0:T(8,128)(2,1)S(1)}) custom-call(s32[1]{0:T(128)} %bitcast.13.first_ref, s32[8]{0:T(128)S(1)} %copy-done.19, s32[4,8]{1,0:T(4,128)S(1)} %bitcast.37, bf16[24,1408]{1,0:T(8,128)(2,1)S(1)} %shard_map.287.own_ref, ...), custom_call_target="tpu_custom_call" | custom-call | flops 3000000000 | bytes 8388608 | tf_op jit(solution)/shard_map/pallas_call | solution.py:48
  91.7 2.9 %collective-permute-start.12 = (bf16[9,24,128]{2,1,0:T(8,128)(2,1)S(1)}, bf16[9,24,128]{2,1,0:T(8,128)(2,1)S(1)}, u32[]{:S(2)}, u32[]{:S(2)}) collective-permute-start(bf16[9,24,128]{2,1,0:T(8,128)(2,1)S(1)} %get-tuple-element.28.refs_0_), channel_id=1, source_target_pairs={{0,16},{8,24},{16,0},{24,8},{1,17},{9,25},{17,1},{25,9},{2,18},{10... | collective-permute-start | bytes 165896 | tf_op jit(solution)/shard_map/ppermute | solution.py:34
  94.5 1.8 %collective-permute-start.13 = (bf16[9,24,128]{2,1,0:T(8,128)(2,1)S(1)}, bf16[9,24,128]{2,1,0:T(8,128)(2,1)S(1)}, u32[]{:S(2)}, u32[]{:S(2)}) collective-permute-start(bf16[9,24,128]{2,1,0:T(8,128)(2,1)S(1)} %get-tuple-element.28.refs_0_), channel_id=1, source_target_pairs={{0,24},{8,16},{16,8},{24,0},{1,25},{9,17},{17,9},{25,1},{2,26},{10... | collective-permute-start | bytes 165896 | tf_op jit(solution)/shard_map/ppermute | solution.py:34
  97.3 2.6 %collective-permute-done.13.refs_3_ = bf16[9,24,128]{2,1,0:T(8,128)(2,1)S(1)} collective-permute-done((bf16[9,24,128]{2,1,0:T(8,128)(2,1)S(1)}, bf16[9,24,128]{2,1,0:T(8,128)(2,1)S(1)}, u32[]{:S(2)}, u32[]{:S(2)}) %collective-permute-start.13) | collective-permute-done | bytes 55328 | tf_op jit(solution)/shard_map/ppermute | solution.py:34
  100.2 1.4 %collective-permute-start.14 = (bf16[9,24,128]{2,1,0:T(8,128)(2,1)S(1)}, bf16[9,24,128]{2,1,0:T(8,128)(2,1)S(1)}, u32[]{:S(2)}, u32[]{:S(2)}) collective-permute-start(bf16[9,24,128]{2,1,0:T(8,128)(2,1)S(1)} %shard_map.289.refs_0_), channel_id=1, source_target_pairs={{0,32},{32,0},{1,33},{33,1},{2,34},{34,2},{3,35},{35,3},{4,36},{36... | collective-permute-start | bytes 165896 | tf_op jit(solution)/shard_map/ppermute | solution.py:40
  101.6 2.8 %collective-permute-done.14.refs_1_ = bf16[9,24,128]{2,1,0:T(8,128)(2,1)S(1)} collective-permute-done((bf16[9,24,128]{2,1,0:T(8,128)(2,1)S(1)}, bf16[9,24,128]{2,1,0:T(8,128)(2,1)S(1)}, u32[]{:S(2)}, u32[]{:S(2)}) %collective-permute-start.14) | collective-permute-done | bytes 55328 | tf_op jit(solution)/shard_map/ppermute | solution.py:40
  104.7 1.8 %collective-permute-start.15 = (bf16[9,24,128]{2,1,0:T(8,128)(2,1)S(1)}, bf16[9,24,128]{2,1,0:T(8,128)(2,1)S(1)}, u32[]{:S(2)}, u32[]{:S(2)}) collective-permute-start(bf16[9,24,128]{2,1,0:T(8,128)(2,1)S(1)} %shard_map.290.own_ref), channel_id=1, source_target_pairs={{0,64},{64,0},{128,192},{192,128},{1,65},{65,1},{129,193},{193,129... | collective-permute-start | bytes 165896 | tf_op jit(solution)/shard_map/ppermute | solution.py:34
  106.5 4.2 %collective-permute-start.16 = (bf16[9,24,128]{2,1,0:T(8,128)(2,1)S(1)}, bf16[9,24,128]{2,1,0:T(8,128)(2,1)S(1)}, u32[]{:S(2)}, u32[]{:S(2)}) collective-permute-start(bf16[9,24,128]{2,1,0:T(8,128)(2,1)S(1)} %shard_map.290.own_ref), channel_id=1, source_target_pairs={{0,128},{64,192},{128,0},{192,64},{1,129},{65,193},{129,1},{193,65... | collective-permute-start | bytes 165896 | tf_op jit(solution)/shard_map/ppermute | solution.py:34
  111.3 3.3 %collective-permute-done.16.two_ref = bf16[9,24,128]{2,1,0:T(8,128)(2,1)S(1)} collective-permute-done((bf16[9,24,128]{2,1,0:T(8,128)(2,1)S(1)}, bf16[9,24,128]{2,1,0:T(8,128)(2,1)S(1)}, u32[]{:S(2)}, u32[]{:S(2)}) %collective-permute-start.16) | collective-permute-done | bytes 55328 | tf_op jit(solution)/shard_map/ppermute | solution.py:34
  114.6 2.4 %collective-permute-done.17.three_ref = bf16[9,24,128]{2,1,0:T(8,128)(2,1)S(1)} collective-permute-done((bf16[9,24,128]{2,1,0:T(8,128)(2,1)S(1)}, bf16[9,24,128]{2,1,0:T(8,128)(2,1)S(1)}, u32[]{:S(2)}, u32[]{:S(2)}) %collective-permute-start.17) | collective-permute-done | bytes 55328 | tf_op jit(solution)/shard_map/ppermute | solution.py:34
  117.4 1.2 collective-permute-done.18
  119.2 2.0 %collective-permute-start.20 = (bf16[24,256]{1,0:T(8,128)(2,1)S(1)}, bf16[24,256]{1,0:T(8,128)(2,1)S(1)}, u32[]{:S(2)}, u32[]{:S(2)}) collective-permute-start(bf16[24,256]{1,0:T(8,128)(2,1)S(1)} %add.27), channel_id=1, source_target_pairs={{0,4},{2,6},{4,0},{6,2},{1,5},{3,7},{5,1},{7,3},{8,12},{10,14},{12... | collective-permute-start | bytes 36872 | tf_op jit(solution)/shard_map/ppermute | solution.py:34
  121.3 2.1 %collective-permute-start.21 = (bf16[24,256]{1,0:T(8,128)(2,1)S(1)}, bf16[24,256]{1,0:T(8,128)(2,1)S(1)}, u32[]{:S(2)}, u32[]{:S(2)}) collective-permute-start(bf16[24,256]{1,0:T(8,128)(2,1)S(1)} %add.27), channel_id=1, source_target_pairs={{0,6},{2,4},{4,2},{6,0},{1,7},{3,5},{5,3},{7,1},{8,14},{10,12},{12... | collective-permute-start | bytes 36872 | tf_op jit(solution)/shard_map/ppermute | solution.py:34
  124.4 1.8 %collective-permute-done.21 = bf16[24,256]{1,0:T(8,128)(2,1)S(1)} collective-permute-done((bf16[24,256]{1,0:T(8,128)(2,1)S(1)}, bf16[24,256]{1,0:T(8,128)(2,1)S(1)}, u32[]{:S(2)}, u32[]{:S(2)}) %collective-permute-start.21) | collective-permute-done | bytes 12320 | tf_op jit(solution)/shard_map/ppermute | solution.py:34
  (75 shorter events, 10.2 us)
Async XLA Ops:
  26.0 15.1 %copy-start = (bf16[2048,544]{0,1:T(8,128)(2,1)S(1)}, bf16[2048,544]{0,1:T(8,128)(2,1)}, u32[]{:S(2)}) copy-start(bf16[2048,544]{0,1:T(8,128)(2,1)} %param.32) | copy-start | bytes 6684676
  26.0 15.1 %copy-start.5 = (f32[8,3,2048]{2,0,1:T(8,128)S(1)}, f32[8,3,2048]{2,0,1:T(8,128)}, u32[]{:S(2)}) copy-start(f32[8,3,2048]{2,0,1:T(8,128)} %param.50) | copy-start | bytes 589828
  26.0 15.1 %copy-start.9 = (f32[4,2048]{1,0:T(4,128)S(1)}, f32[4,2048]{1,0:T(4,128)}, u32[]{:S(2)}) copy-start(f32[4,2048]{1,0:T(4,128)} %taps_ref.1) | copy-start | bytes 98308
  26.0 15.1 %copy-start.11 = (f32[2048]{0:T(1024)S(1)}, f32[2048]{0:T(1024)}, u32[]{:S(2)}) copy-start(f32[2048]{0:T(1024)} %param.31) | copy-start | bytes 24580
  42.5 1.3 %collective-permute-start = (bf16[24,544]{1,0:T(8,128)(2,1)S(1)}, bf16[24,544]{1,0:T(8,128)(2,1)S(1)}, u32[]{:S(2)}, u32[]{:S(2)}) collective-permute-start(bf16[24,544]{1,0:T(8,128)(2,1)S(1)} %get-tuple-element.19), channel_id=1, source_target_pairs={{0,1},{1,0},{2,3},{3,2},{4,5},{5,4},{6,7},{7,6},{8,9},{9,8},{10,11... | collective-permute-start | bytes 78344 | tf_op jit(solution)/shard_map/ppermute | solution.py:40
  43.8 6.6 %collective-permute-start.1 = (bf16[24,544]{1,0:T(8,128)(2,1)S(1)}, bf16[24,544]{1,0:T(8,128)(2,1)S(1)}, u32[]{:S(2)}, u32[]{:S(2)}) collective-permute-start(bf16[24,544]{1,0:T(8,128)(2,1)S(1)} %add.24.own_ref), channel_id=1, source_target_pairs={{0,2},{2,0},{4,6},{6,4},{1,3},{3,1},{5,7},{7,5},{8,10},{10,8},{12,... | collective-permute-start | bytes 78344 | tf_op jit(solution)/shard_map/ppermute | solution.py:34
  45.5 5.4 %collective-permute-start.2 = (bf16[24,544]{1,0:T(8,128)(2,1)S(1)}, bf16[24,544]{1,0:T(8,128)(2,1)S(1)}, u32[]{:S(2)}, u32[]{:S(2)}) collective-permute-start(bf16[24,544]{1,0:T(8,128)(2,1)S(1)} %add.24.own_ref), channel_id=1, source_target_pairs={{0,4},{2,6},{4,0},{6,2},{1,5},{3,7},{5,1},{7,3},{8,12},{10,14},{12... | collective-permute-start | bytes 78344 | tf_op jit(solution)/shard_map/ppermute | solution.py:34
  48.4 5.1 %collective-permute-start.3 = (bf16[24,544]{1,0:T(8,128)(2,1)S(1)}, bf16[24,544]{1,0:T(8,128)(2,1)S(1)}, u32[]{:S(2)}, u32[]{:S(2)}) collective-permute-start(bf16[24,544]{1,0:T(8,128)(2,1)S(1)} %add.24.own_ref), channel_id=1, source_target_pairs={{0,6},{2,4},{4,2},{6,0},{1,7},{3,5},{5,3},{7,1},{8,14},{10,12},{12... | collective-permute-start | bytes 78344 | tf_op jit(solution)/shard_map/ppermute | solution.py:34
  53.5 12.3 %copy-start.3 = (bf16[256,1024]{1,0:T(8,128)(2,1)S(1)}, bf16[256,1024]{1,0:T(8,128)(2,1)}, u32[]{:S(2)}) copy-start(bf16[256,1024]{1,0:T(8,128)(2,1)} %wq_ref.1) | copy-start | bytes 1572868
  53.5 12.3 %copy-start.7 = (bf16[256,128]{1,0:T(8,128)(2,1)S(1)}, bf16[256,128]{1,0:T(8,128)(2,1)}, u32[]{:S(2)}) copy-start(bf16[256,128]{1,0:T(8,128)(2,1)} %wk_ref.1) | copy-start | bytes 196612
  53.6 12.3 %copy-start.8 = (bf16[256,128]{1,0:T(8,128)(2,1)S(1)}, bf16[256,128]{1,0:T(8,128)(2,1)}, u32[]{:S(2)}) copy-start(bf16[256,128]{1,0:T(8,128)(2,1)} %wv_ref.1) | copy-start | bytes 196612
  53.6 12.3 %copy-start.10 = (bf16[3,8,256]{2,1,0:T(8,128)(2,1)S(1)}, bf16[3,8,256]{2,1,0:T(8,128)(2,1)}, u32[]{:S(2)}) copy-start(bf16[3,8,256]{2,1,0:T(8,128)(2,1)} %param.26) | copy-start | bytes 36868
  53.6 12.3 %copy-start.16 = (f32[256]{0:T(256)S(1)}, f32[256]{0:T(256)}, u32[]{:S(2)}) copy-start(f32[256]{0:T(256)} %param.41) | copy-start | bytes 3076
  66.1 4.8 %collective-permute-start.4 = (bf16[24,1408]{1,0:T(8,128)(2,1)S(1)}, bf16[24,1408]{1,0:T(8,128)(2,1)S(1)}, u32[]{:S(2)}, u32[]{:S(2)}) collective-permute-start(bf16[24,1408]{1,0:T(8,128)(2,1)S(1)} %get-tuple-element.23.refs_0_), channel_id=1, source_target_pairs={{0,8},{8,0},{16,24},{24,16},{1,9},{9,1},{17,25},{25,17},{2,10},{10... | collective-permute-start | bytes 202760 | tf_op jit(solution)/shard_map/ppermute | solution.py:34
  66.7 6.2 %collective-permute-start.5 = (bf16[24,1408]{1,0:T(8,128)(2,1)S(1)}, bf16[24,1408]{1,0:T(8,128)(2,1)S(1)}, u32[]{:S(2)}, u32[]{:S(2)}) collective-permute-start(bf16[24,1408]{1,0:T(8,128)(2,1)S(1)} %get-tuple-element.23.refs_0_), channel_id=1, source_target_pairs={{0,16},{8,24},{16,0},{24,8},{1,17},{9,25},{17,1},{25,9},{2,18},{10... | collective-permute-start | bytes 202760 | tf_op jit(solution)/shard_map/ppermute | solution.py:34
  69.7 5.5 %collective-permute-start.6 = (bf16[24,1408]{1,0:T(8,128)(2,1)S(1)}, bf16[24,1408]{1,0:T(8,128)(2,1)S(1)}, u32[]{:S(2)}, u32[]{:S(2)}) collective-permute-start(bf16[24,1408]{1,0:T(8,128)(2,1)S(1)} %get-tuple-element.23.refs_0_), channel_id=1, source_target_pairs={{0,24},{8,16},{16,8},{24,0},{1,25},{9,17},{17,9},{25,1},{2,26},{10... | collective-permute-start | bytes 202760 | tf_op jit(solution)/shard_map/ppermute | solution.py:34
  75.3 4.6 %collective-permute-start.7 = (bf16[24,1408]{1,0:T(8,128)(2,1)S(1)}, bf16[24,1408]{1,0:T(8,128)(2,1)S(1)}, u32[]{:S(2)}, u32[]{:S(2)}) collective-permute-start(bf16[24,1408]{1,0:T(8,128)(2,1)S(1)} %shard_map.286.refs_0_), channel_id=1, source_target_pairs={{0,32},{32,0},{1,33},{33,1},{2,34},{34,2},{3,35},{35,3},{4,36},{36... | collective-permute-start | bytes 202760 | tf_op jit(solution)/shard_map/ppermute | solution.py:40
  80.1 9.6 %collective-permute-start.10 = (bf16[24,1408]{1,0:T(8,128)(2,1)S(1)}, bf16[24,1408]{1,0:T(8,128)(2,1)S(1)}, u32[]{:S(2)}, u32[]{:S(2)}) collective-permute-start(bf16[24,1408]{1,0:T(8,128)(2,1)S(1)} %shard_map.287.own_ref), channel_id=1, source_target_pairs={{0,192},{64,128},{128,64},{192,0},{1,193},{65,129},{129,65},{193,1... | collective-permute-start | bytes 202760 | tf_op jit(solution)/shard_map/ppermute | solution.py:34
  80.5 9.2 %collective-permute-start.8 = (bf16[24,1408]{1,0:T(8,128)(2,1)S(1)}, bf16[24,1408]{1,0:T(8,128)(2,1)S(1)}, u32[]{:S(2)}, u32[]{:S(2)}) collective-permute-start(bf16[24,1408]{1,0:T(8,128)(2,1)S(1)} %shard_map.287.own_ref), channel_id=1, source_target_pairs={{0,64},{64,0},{128,192},{192,128},{1,65},{65,1},{129,193},{193,129... | collective-permute-start | bytes 202760 | tf_op jit(solution)/shard_map/ppermute | solution.py:34
  81.4 8.4 %collective-permute-start.9 = (bf16[24,1408]{1,0:T(8,128)(2,1)S(1)}, bf16[24,1408]{1,0:T(8,128)(2,1)S(1)}, u32[]{:S(2)}, u32[]{:S(2)}) collective-permute-start(bf16[24,1408]{1,0:T(8,128)(2,1)S(1)} %shard_map.287.own_ref), channel_id=1, source_target_pairs={{0,128},{64,192},{128,0},{192,64},{1,129},{65,193},{129,1},{193,65... | collective-permute-start | bytes 202760 | tf_op jit(solution)/shard_map/ppermute | solution.py:34
  91.7 4.7 %collective-permute-start.11 = (bf16[9,24,128]{2,1,0:T(8,128)(2,1)S(1)}, bf16[9,24,128]{2,1,0:T(8,128)(2,1)S(1)}, u32[]{:S(2)}, u32[]{:S(2)}) collective-permute-start(bf16[9,24,128]{2,1,0:T(8,128)(2,1)S(1)} %get-tuple-element.28.refs_0_), channel_id=1, source_target_pairs={{0,8},{8,0},{16,24},{24,16},{1,9},{9,1},{17,25},{25,17},{2,10},{10... | collective-permute-start | bytes 165896 | tf_op jit(solution)/shard_map/ppermute | solution.py:34
  91.7 5.7 %collective-permute-start.12 = (bf16[9,24,128]{2,1,0:T(8,128)(2,1)S(1)}, bf16[9,24,128]{2,1,0:T(8,128)(2,1)S(1)}, u32[]{:S(2)}, u32[]{:S(2)}) collective-permute-start(bf16[9,24,128]{2,1,0:T(8,128)(2,1)S(1)} %get-tuple-element.28.refs_0_), channel_id=1, source_target_pairs={{0,16},{8,24},{16,0},{24,8},{1,17},{9,25},{17,1},{25,9},{2,18},{10... | collective-permute-start | bytes 165896 | tf_op jit(solution)/shard_map/ppermute | solution.py:34
  94.5 5.4 %collective-permute-start.13 = (bf16[9,24,128]{2,1,0:T(8,128)(2,1)S(1)}, bf16[9,24,128]{2,1,0:T(8,128)(2,1)S(1)}, u32[]{:S(2)}, u32[]{:S(2)}) collective-permute-start(bf16[9,24,128]{2,1,0:T(8,128)(2,1)S(1)} %get-tuple-element.28.refs_0_), channel_id=1, source_target_pairs={{0,24},{8,16},{16,8},{24,0},{1,25},{9,17},{17,9},{25,1},{2,26},{10... | collective-permute-start | bytes 165896 | tf_op jit(solution)/shard_map/ppermute | solution.py:34
  100.2 16.8 %copy-start.4 = (bf16[1024,256]{1,0:T(8,128)(2,1)S(1)}, bf16[1024,256]{1,0:T(8,128)(2,1)}, u32[]{:S(2)}) copy-start(bf16[1024,256]{1,0:T(8,128)(2,1)} %weight_ref.1) | copy-start | bytes 1572868
  100.2 4.2 %collective-permute-start.14 = (bf16[9,24,128]{2,1,0:T(8,128)(2,1)S(1)}, bf16[9,24,128]{2,1,0:T(8,128)(2,1)S(1)}, u32[]{:S(2)}, u32[]{:S(2)}) collective-permute-start(bf16[9,24,128]{2,1,0:T(8,128)(2,1)S(1)} %shard_map.289.refs_0_), channel_id=1, source_target_pairs={{0,32},{32,0},{1,33},{33,1},{2,34},{34,2},{3,35},{35,3},{4,36},{36... | collective-permute-start | bytes 165896 | tf_op jit(solution)/shard_map/ppermute | solution.py:40
  104.7 6.6 %collective-permute-start.15 = (bf16[9,24,128]{2,1,0:T(8,128)(2,1)S(1)}, bf16[9,24,128]{2,1,0:T(8,128)(2,1)S(1)}, u32[]{:S(2)}, u32[]{:S(2)}) collective-permute-start(bf16[9,24,128]{2,1,0:T(8,128)(2,1)S(1)} %shard_map.290.own_ref), channel_id=1, source_target_pairs={{0,64},{64,0},{128,192},{192,128},{1,65},{65,1},{129,193},{193,129... | collective-permute-start | bytes 165896 | tf_op jit(solution)/shard_map/ppermute | solution.py:34
  106.5 8.1 %collective-permute-start.16 = (bf16[9,24,128]{2,1,0:T(8,128)(2,1)S(1)}, bf16[9,24,128]{2,1,0:T(8,128)(2,1)S(1)}, u32[]{:S(2)}, u32[]{:S(2)}) collective-permute-start(bf16[9,24,128]{2,1,0:T(8,128)(2,1)S(1)} %shard_map.290.own_ref), channel_id=1, source_target_pairs={{0,128},{64,192},{128,0},{192,64},{1,129},{65,193},{129,1},{193,65... | collective-permute-start | bytes 165896 | tf_op jit(solution)/shard_map/ppermute | solution.py:34
  110.7 6.3 %collective-permute-start.17 = (bf16[9,24,128]{2,1,0:T(8,128)(2,1)S(1)}, bf16[9,24,128]{2,1,0:T(8,128)(2,1)S(1)}, u32[]{:S(2)}, u32[]{:S(2)}) collective-permute-start(bf16[9,24,128]{2,1,0:T(8,128)(2,1)S(1)} %shard_map.290.own_ref), channel_id=1, source_target_pairs={{0,192},{64,128},{128,64},{192,0},{1,193},{65,129},{129,65},{193,1... | collective-permute-start | bytes 165896 | tf_op jit(solution)/shard_map/ppermute | solution.py:34
  117.4 1.2 collective-permute-start.18
  118.6 4.7 %collective-permute-start.19 = (bf16[24,256]{1,0:T(8,128)(2,1)S(1)}, bf16[24,256]{1,0:T(8,128)(2,1)S(1)}, u32[]{:S(2)}, u32[]{:S(2)}) collective-permute-start(bf16[24,256]{1,0:T(8,128)(2,1)S(1)} %add.27), channel_id=1, source_target_pairs={{0,2},{2,0},{4,6},{6,4},{1,3},{3,1},{5,7},{7,5},{8,10},{10,8},{12,... | collective-permute-start | bytes 36872 | tf_op jit(solution)/shard_map/ppermute | solution.py:34
  119.2 5.2 %collective-permute-start.20 = (bf16[24,256]{1,0:T(8,128)(2,1)S(1)}, bf16[24,256]{1,0:T(8,128)(2,1)S(1)}, u32[]{:S(2)}, u32[]{:S(2)}) collective-permute-start(bf16[24,256]{1,0:T(8,128)(2,1)S(1)} %add.27), channel_id=1, source_target_pairs={{0,4},{2,6},{4,0},{6,2},{1,5},{3,7},{5,1},{7,3},{8,12},{10,14},{12... | collective-permute-start | bytes 36872 | tf_op jit(solution)/shard_map/ppermute | solution.py:34
  121.3 4.9 %collective-permute-start.21 = (bf16[24,256]{1,0:T(8,128)(2,1)S(1)}, bf16[24,256]{1,0:T(8,128)(2,1)S(1)}, u32[]{:S(2)}, u32[]{:S(2)}) collective-permute-start(bf16[24,256]{1,0:T(8,128)(2,1)S(1)} %add.27), channel_id=1, source_target_pairs={{0,6},{2,4},{4,2},{6,0},{1,7},{3,5},{5,3},{7,1},{8,14},{10,12},{12... | collective-permute-start | bytes 36872 | tf_op jit(solution)/shard_map/ppermute | solution.py:34
  (11 other events, 112.4 us)
where the time goes:
time: 129 us; the launch traced here: 127 us
  blocking collectives  45.9 us (36%)
  starting transfers between devices  34.3 us (27%)
  waiting for transfers between devices  28.8 us (22%)
  Pallas kernels  11.4 us (9%)
  local copies, waits for them, and re-layouts  4.84 us (4%)
    all_to_all x3, blocking collectives, exchange(): return lax.all_to_all(parts, axis, 0, 0, tiled=True)  45.9 us
    ppermute x18, starting transfers between devices, from_partners(): lax.ppermute(part, axis, [(i, i ^ flip) for i in range(4)])  32.1 us
    ppermute x18, waiting for transfers between devices, from_partners(): lax.ppermute(part, axis, [(i, i ^ flip) for i in range(4)])  19.6 us
    pallas_call x11, Pallas kernels, call(): pl.pallas_call(kernel, out_shape=[jax.ShapeDtypeStruct(shape, dtype) for...  11.4 us
    ppermute x4, waiting for transfers between devices, from_other(): return lax.ppermute(part, axis, [(0, 1), (1, 0)])  9.13 us
  transfers between devices with their start and end apart: 22, of which 15 were waited for; matrix products, arithmetic and copies ran while one was open for 4% of the time, Pallas kernels for 0%

commit v1 on v0

--- a/solution.py
+++ b/solution.py
@@ -19,7 +19,6 @@
 CTX = ("za", "zb", "x")
 TP = ("y", "core")
 FLOPS = 3_000_000_000
-GROUPS = 4
 NEGATIVE = -1e30
 bf16 = jnp.bfloat16
 f32 = jnp.float32
@@ -139,25 +138,9 @@
 
 def scan_kernel(
     own_ref, one_ref, two_ref, three_ref, dt_gain_ref, b_gain_ref, c_gain_ref, dt_bias_ref, a_ref, skip_ref, mixed_ref, gate_ref,
-    state_hbm, dtp_hbm, op_hbm, state_out_hbm, part_ref,
-    dtp_ref, op_ref, state_ref, b_wide, c_wide, decay_wide, sems, state_sems,
+    state_ref, dtp_ref, op_ref, state_out_ref, part_ref, b_wide, c_wide, decay_wide,
 ):
     tiles = state_ref.shape[0]
-    group = tiles // GROUPS
-    dtp_copy = pltpu.make_async_copy(dtp_hbm, dtp_ref, sems.at[0])
-    op_copy = pltpu.make_async_copy(op_hbm, op_ref, sems.at[1])
-    dtp_copy.start()
-    entering, leaving = [], []
-    for i in range(GROUPS):
-        at = pl.ds(i * group, group)
-        entering.append(
-            pltpu.make_async_copy(state_hbm.at[at], state_ref.at[at], state_sems.at[0, i])
-        )
-        entering[i].start()
-        leaving.append(
-            pltpu.make_async_copy(state_ref.at[at], state_out_hbm.at[at], state_sems.at[1, i])
-        )
-    op_copy.start()
     low = sum_refs((own_ref, one_ref, two_ref, three_ref))
     raw = low[:, :DTR]
     mean_sq = jnp.sum(raw * raw, axis=1, keepdims=True) / DTR
@@ -172,7 +155,6 @@
         decay = -jnp.exp(a_ref[:, tile * LANES : (tile + 1) * LANES])
         for n in range(DS):
             decay_wide[tile, n] = jnp.broadcast_to(decay[n : n + 1], (ROWS, LANES))
-    dtp_copy.wait()
     raw = jnp.dot(dt_low, dtp_ref[...], preferred_element_type=f32) + dt_bias_ref[...]
     steps = jnp.maximum(raw, 0.0) + jnp.log1p(jnp.exp(-jnp.abs(raw)))
     mixed = mixed_ref[...]
@@ -180,8 +162,6 @@
     scanned = []
     for tile in range(tiles):
         cols = slice(tile * LANES, (tile + 1) * LANES)
-        if tile % group == 0:
-            entering[tile // group].wait()
         y = [jnp.zeros((ROWS, LANES), f32) for _ in range(STEPS)]
         for n in range(DS):
             state = state_ref[tile, n]
@@ -192,18 +172,13 @@
                     jnp.exp(steps[rows, cols] * decay) * state + drive[rows, cols] * b_wide[n, rows]
                 )
                 y[s] = y[s] + c_wide[n, rows] * state
-            state_ref[tile, n] = state
-        if tile % group == group - 1:
-            leaving[tile // group].start()
+            state_out_ref[tile, n] = state
         y = jnp.concatenate(y, axis=0) + skip_ref[:, cols] * mixed[:, cols]
         scanned.append((y * silu(gate_ref[tiles + tile].astype(f32))).astype(bf16))
-    op_copy.wait()
     total = jnp.dot(jnp.concatenate(scanned, axis=1), op_ref[...], preferred_element_type=f32)
     part = total.astype(bf16)
     for target in range(part_ref.shape[0]):
         part_ref[target] = part
-    for copy in leaving:
-        copy.wait()
 
 
 def qkv_kernel(parts_ref, rows_ref, gain_ref, wq_ref, wk_ref, wv_ref, residual_ref, out_ref):
@@ -467,18 +442,10 @@
         state,
         dt_proj,
         out_proj,
-        vmem_mib=53,
-        in_specs=[vmem] * 12 + [hbm] * 3,
-        out_specs=[hbm, vmem],
         scratch_shapes=[
-            pltpu.VMEM(dt_proj.shape, bf16),
-            pltpu.VMEM(out_proj.shape, bf16),
-            pltpu.VMEM(tiled, f32),
             pltpu.VMEM((DS, ALL_ROWS, LANES), f32),
             pltpu.VMEM((DS, ALL_ROWS, LANES), f32),
             pltpu.VMEM(tiled, f32),
-            pltpu.SemaphoreType.DMA((2,)),
-            pltpu.SemaphoreType.DMA((2, GROUPS)),
         ],
     )
     state = state.transpose(2, 1, 0, 3).reshape(ssm_state.shape)

time: 129 us -> 126 us (0.977)
  Pallas kernels: 11.4 us -> 8.97 us
    pallas_call x11, Pallas kernels: 11.4 us -> 8.97 us  [call(): pl.pallas_call(kernel, out_shape=[jax.ShapeDtypeStruct(shape, dtype) for...]
  transfers between devices with their start and end apart: 22 -> 22, of which waited for: 15 -> 14; matrix products, arithmetic and copies ran while one was open for 4% -> 4% of each run, Pallas kernels for 0% -> 0%
where the time goes in v1:
time: 126 us; the launch traced here: 124 us
  blocking collectives  45.9 us (36%)
  starting transfers between devices  34 us (27%)
  waiting for transfers between devices  29.1 us (23%)
  Pallas kernels  8.97 us (7%)
  local copies, waits for them, and re-layouts  4.88 us (4%)
    all_to_all x3, blocking collectives, exchange(): return lax.all_to_all(parts, axis, 0, 0, tiled=True)  45.9 us
    ppermute x18, starting transfers between devices, from_partners(): lax.ppermute(part, axis, [(i, i ^ flip) for i in range(4)])  32.1 us
    ppermute x18, waiting for transfers between devices, from_partners(): lax.ppermute(part, axis, [(i, i ^ flip) for i in range(4)])  19.6 us
    ppermute x4, waiting for transfers between devices, from_other(): return lax.ppermute(part, axis, [(0, 1), (1, 0)])  9.51 us
    pallas_call x11, Pallas kernels, call(): pl.pallas_call(kernel, out_shape=[jax.ShapeDtypeStruct(shape, dtype) for...  8.97 us
  transfers between devices with their start and end apart: 22, of which 14 were waited for; matrix products, arithmetic and copies ran while one was open for 4% of the time, Pallas kernels for 0%

profile of v1, /device:TPU:6, one launch (start us, length us, event | category | flops | bytes accessed | tf_op | source)
XLA Modules:
  0.0 124.4 jit_solution(16036391480381362408)
XLA Ops:
  0.6 2.6 %shard_map.281 = bf16[2,16,32,128]{3,2,1,0:T(8,128)(2,1)} custom-call(bf16[24,256]{1,0:T(8,128)(2,1)} %bitcast.33, f32[1,256]{1,0:T(1,128)} %bitcast.46, bf16[256,2048]{1,0:T(8,128)(2,1)} %wx_hbm.1, bf16[256,2048]{1,0:T(8,128)(2,1)} %wz_hbm.1), custom_call_target="tpu_custom_call" | custom-call | flops 3000000000 | bytes 8388608 | tf_op jit(solution)/shard_map/pallas_call | solution.py:47
  3.2 22.8 %all_to_all.15.in_ref = bf16[32,32,128]{2,1,0:T(8,128)(2,1)S(1)} all-to-all(bf16[32,32,128]{2,1,0:T(8,128)(2,1)} %bitcast.45), channel_id=1, replica_groups=mesh['za'=4,'zb'=2,'x'=4,'y'=4,'core'=2] {'za','zb','x'}, dimensions={0} | all-to-all | bytes 524288 | tf_op jit(solution)/shard_map/all_to_all | solution.py:28
  26.2 14.9 %all_to_all.16.inner_ref.gate_ref = bf16[32,24,128]{2,1,0:T(8,128)(2,1)S(1)} all-to-all(bf16[32,24,128]{2,1,0:T(8,128)(2,1)S(1)} %shard_map.282), channel_id=1, replica_groups=mesh['za'=4,'zb'=2,'x'=4,'y'=4,'core'=2] {'za','zb','x'}, dimensions={0} | all-to-all | bytes 393216 | tf_op jit(solution)/shard_map/all_to_all | solution.py:28
  41.1 1.3 %shard_map.283 = (bf16[24,544]{1,0:T(8,128)(2,1)S(1)}, f32[24,2048]{1,0:T(8,128)S(1)}, f32[3,8,2048]{2,1,0:T(8,128)}) custom-call(bf16[32,24,128]{2,1,0:T(8,128)(2,1)S(1)} %all_to_all.16.inner_ref.gate_ref, f32[3,8,2048]{2,1,0:T(8,128)S(1)} %bitcast.32, f32[4,2048]{1,0:T(4,128)S(1)} %copy-done.11, f32[1,2048]{1,0:T(1,128)S(1)} %bitcast.35, ...), custom_call_target="tpu_custom_call" | custom-call | flops 3000000000 | bytes 8388608 | tf_op jit(solution)/shard_map/pallas_call | solution.py:47
  42.6 1.2 collective-permute-done
  43.8 1.7 %collective-permute-start.1 = (bf16[24,544]{1,0:T(8,128)(2,1)S(1)}, bf16[24,544]{1,0:T(8,128)(2,1)S(1)}, u32[]{:S(2)}, u32[]{:S(2)}) collective-permute-start(bf16[24,544]{1,0:T(8,128)(2,1)S(1)} %add.24.own_ref), channel_id=1, source_target_pairs={{0,2},{2,0},{4,6},{6,4},{1,3},{3,1},{5,7},{7,5},{8,10},{10,8},{12,... | collective-permute-start | bytes 78344 | tf_op jit(solution)/shard_map/ppermute | solution.py:33
  45.5 2.9 %collective-permute-start.2 = (bf16[24,544]{1,0:T(8,128)(2,1)S(1)}, bf16[24,544]{1,0:T(8,128)(2,1)S(1)}, u32[]{:S(2)}, u32[]{:S(2)}) collective-permute-start(bf16[24,544]{1,0:T(8,128)(2,1)S(1)} %add.24.own_ref), channel_id=1, source_target_pairs={{0,4},{2,6},{4,0},{6,2},{1,5},{3,7},{5,1},{7,3},{8,12},{10,14},{12... | collective-permute-start | bytes 78344 | tf_op jit(solution)/shard_map/ppermute | solution.py:33
  49.5 1.5 %collective-permute-done.2.two_ref = bf16[24,544]{1,0:T(8,128)(2,1)S(1)} collective-permute-done((bf16[24,544]{1,0:T(8,128)(2,1)S(1)}, bf16[24,544]{1,0:T(8,128)(2,1)S(1)}, u32[]{:S(2)}, u32[]{:S(2)}) %collective-permute-start.2) | collective-permute-done | bytes 26144 | tf_op jit(solution)/shard_map/ppermute | solution.py:33
  50.9 2.6 %collective-permute-done.3.three_ref = bf16[24,544]{1,0:T(8,128)(2,1)S(1)} collective-permute-done((bf16[24,544]{1,0:T(8,128)(2,1)S(1)}, bf16[24,544]{1,0:T(8,128)(2,1)S(1)}, u32[]{:S(2)}, u32[]{:S(2)}) %collective-permute-start.3) | collective-permute-done | bytes 26144 | tf_op jit(solution)/shard_map/ppermute | solution.py:33
  53.6 1.6 %shard_map.284 = (f32[16,16,8,128]{3,2,1,0:T(8,128)S(1)}, bf16[8,24,256]{2,1,0:T(8,128)(2,1)S(1)}) custom-call(bf16[24,544]{1,0:T(8,128)(2,1)S(1)} %add.24.own_ref, bf16[24,544]{1,0:T(8,128)(2,1)S(1)} %collective-permute-done.1.one_ref, bf16[24,544]{1,0:T(8,128)(2,1)S(1)} %collective-permute-done.2.two_ref, ...), custom_call_target="tpu_custom_call" | custom-call | flops 3000000000 | bytes 8388608 | tf_op jit(solution)/shard_map/pallas_call | solution.py:47
  55.3 8.2 %all_to_all.17.parts_ref = bf16[8,24,256]{2,1,0:T(8,128)(2,1)S(1)} all-to-all(bf16[8,24,256]{2,1,0:T(8,128)(2,1)S(1)} %get-tuple-element.21), channel_id=1, replica_groups=mesh['za'=4,'zb'=2,'x'=4,'y'=4,'core'=2] {'y','core'}, dimensions={0} | all-to-all | bytes 196608 | tf_op jit(solution)/shard_map/all_to_all | solution.py:28
  64.3 3.0 %collective-permute-start.5 = (bf16[24,1408]{1,0:T(8,128)(2,1)S(1)}, bf16[24,1408]{1,0:T(8,128)(2,1)S(1)}, u32[]{:S(2)}, u32[]{:S(2)}) collective-permute-start(bf16[24,1408]{1,0:T(8,128)(2,1)S(1)} %get-tuple-element.23.refs_0_), channel_id=1, source_target_pairs={{0,16},{8,24},{16,0},{24,8},{1,17},{9,25},{17,1},{25,9},{2,18},{10... | collective-permute-start | bytes 202760 | tf_op jit(solution)/shard_map/ppermute | solution.py:33
  67.3 1.2 collective-permute-start.6
  68.5 2.0 %collective-permute-done.5.refs_2_ = bf16[24,1408]{1,0:T(8,128)(2,1)S(1)} collective-permute-done((bf16[24,1408]{1,0:T(8,128)(2,1)S(1)}, bf16[24,1408]{1,0:T(8,128)(2,1)S(1)}, u32[]{:S(2)}, u32[]{:S(2)}) %collective-permute-start.5) | collective-permute-done | bytes 67616 | tf_op jit(solution)/shard_map/ppermute | solution.py:33
  70.5 2.3 %collective-permute-done.6.refs_3_ = bf16[24,1408]{1,0:T(8,128)(2,1)S(1)} collective-permute-done((bf16[24,1408]{1,0:T(8,128)(2,1)S(1)}, bf16[24,1408]{1,0:T(8,128)(2,1)S(1)}, u32[]{:S(2)}, u32[]{:S(2)}) %collective-permute-start.6) | collective-permute-done | bytes 67616 | tf_op jit(solution)/shard_map/ppermute | solution.py:33
  73.6 3.9 %collective-permute-done.7.refs_1_ = bf16[24,1408]{1,0:T(8,128)(2,1)S(1)} collective-permute-done((bf16[24,1408]{1,0:T(8,128)(2,1)S(1)}, bf16[24,1408]{1,0:T(8,128)(2,1)S(1)}, u32[]{:S(2)}, u32[]{:S(2)}) %collective-permute-start.7) | collective-permute-done | bytes 67616 | tf_op jit(solution)/shard_map/ppermute | solution.py:39
  79.0 5.3 %collective-permute-start.9 = (bf16[24,1408]{1,0:T(8,128)(2,1)S(1)}, bf16[24,1408]{1,0:T(8,128)(2,1)S(1)}, u32[]{:S(2)}, u32[]{:S(2)}) collective-permute-start(bf16[24,1408]{1,0:T(8,128)(2,1)S(1)} %shard_map.287.own_ref), channel_id=1, source_target_pairs={{0,128},{64,192},{128,0},{192,64},{1,129},{65,193},{129,1},{193,65... | collective-permute-start | bytes 202760 | tf_op jit(solution)/shard_map/ppermute | solution.py:33
  84.3 1.6 %copy.32 = f32[8,16,16,128]{3,2,1,0:T(8,128)} copy(f32[8,16,16,128]{3,0,1,2:T(8,128)S(1)} %bitcast.29) | data formatting | bytes 2097152 | tf_op jit(solution)/shard_map/transpose | solution.py:451
  85.9 2.4 %reshape.73 = f32[8,16,2048]{2,1,0:T(8,128)} reshape(f32[8,16,16,128]{3,2,1,0:T(8,128)} %copy.32) | data formatting | bytes 2097152 | tf_op jit(solution)/shard_map/reshape | solution.py:451
  88.3 1.9 %shard_map.288 = (bf16[24,128]{1,0:T(8,128)(2,1)}, bf16[24,128]{1,0:T(8,128)(2,1)}, bf16[9,24,128]{2,1,0:T(8,128)(2,1)S(1)}) custom-call(s32[1]{0:T(128)} %bitcast.13.first_ref, s32[8]{0:T(128)S(1)} %copy-done.21, s32[4,8]{1,0:T(4,128)S(1)} %bitcast.39, bf16[24,1408]{1,0:T(8,128)(2,1)S(1)} %shard_map.287.own_ref, ...), custom_call_target="tpu_custom_call" | custom-call | flops 3000000000 | bytes 8388608 | tf_op jit(solution)/shard_map/pallas_call | solution.py:47
  90.2 2.4 %collective-permute-start.12 = (bf16[9,24,128]{2,1,0:T(8,128)(2,1)S(1)}, bf16[9,24,128]{2,1,0:T(8,128)(2,1)S(1)}, u32[]{:S(2)}, u32[]{:S(2)}) collective-permute-start(bf16[9,24,128]{2,1,0:T(8,128)(2,1)S(1)} %get-tuple-element.28.refs_0_), channel_id=1, source_target_pairs={{0,16},{8,24},{16,0},{24,8},{1,17},{9,25},{17,1},{25,9},{2,18},{10... | collective-permute-start | bytes 165896 | tf_op jit(solution)/shard_map/ppermute | solution.py:33
  92.5 2.3 %collective-permute-start.13 = (bf16[9,24,128]{2,1,0:T(8,128)(2,1)S(1)}, bf16[9,24,128]{2,1,0:T(8,128)(2,1)S(1)}, u32[]{:S(2)}, u32[]{:S(2)}) collective-permute-start(bf16[9,24,128]{2,1,0:T(8,128)(2,1)S(1)} %get-tuple-element.28.refs_0_), channel_id=1, source_target_pairs={{0,24},{8,16},{16,8},{24,0},{1,25},{9,17},{17,9},{25,1},{2,26},{10... | collective-permute-start | bytes 165896 | tf_op jit(solution)/shard_map/ppermute | solution.py:33
  95.8 2.1 %collective-permute-done.13.refs_3_ = bf16[9,24,128]{2,1,0:T(8,128)(2,1)S(1)} collective-permute-done((bf16[9,24,128]{2,1,0:T(8,128)(2,1)S(1)}, bf16[9,24,128]{2,1,0:T(8,128)(2,1)S(1)}, u32[]{:S(2)}, u32[]{:S(2)}) %collective-permute-start.13) | collective-permute-done | bytes 55328 | tf_op jit(solution)/shard_map/ppermute | solution.py:33
  99.2 3.2 %collective-permute-done.14.refs_1_ = bf16[9,24,128]{2,1,0:T(8,128)(2,1)S(1)} collective-permute-done((bf16[9,24,128]{2,1,0:T(8,128)(2,1)S(1)}, bf16[9,24,128]{2,1,0:T(8,128)(2,1)S(1)}, u32[]{:S(2)}, u32[]{:S(2)}) %collective-permute-start.14) | collective-permute-done | bytes 55328 | tf_op jit(solution)/shard_map/ppermute | solution.py:39
  102.7 1.4 %collective-permute-start.15 = (bf16[9,24,128]{2,1,0:T(8,128)(2,1)S(1)}, bf16[9,24,128]{2,1,0:T(8,128)(2,1)S(1)}, u32[]{:S(2)}, u32[]{:S(2)}) collective-permute-start(bf16[9,24,128]{2,1,0:T(8,128)(2,1)S(1)} %shard_map.290.own_ref), channel_id=1, source_target_pairs={{0,64},{64,0},{128,192},{192,128},{1,65},{65,1},{129,193},{193,129... | collective-permute-start | bytes 165896 | tf_op jit(solution)/shard_map/ppermute | solution.py:33
  104.1 4.2 %collective-permute-start.16 = (bf16[9,24,128]{2,1,0:T(8,128)(2,1)S(1)}, bf16[9,24,128]{2,1,0:T(8,128)(2,1)S(1)}, u32[]{:S(2)}, u32[]{:S(2)}) collective-permute-start(bf16[9,24,128]{2,1,0:T(8,128)(2,1)S(1)} %shard_map.290.own_ref), channel_id=1, source_target_pairs={{0,128},{64,192},{128,0},{192,64},{1,129},{65,193},{129,1},{193,65... | collective-permute-start | bytes 165896 | tf_op jit(solution)/shard_map/ppermute | solution.py:33
  109.2 2.9 %collective-permute-done.16.two_ref = bf16[9,24,128]{2,1,0:T(8,128)(2,1)S(1)} collective-permute-done((bf16[9,24,128]{2,1,0:T(8,128)(2,1)S(1)}, bf16[9,24,128]{2,1,0:T(8,128)(2,1)S(1)}, u32[]{:S(2)}, u32[]{:S(2)}) %collective-permute-start.16) | collective-permute-done | bytes 55328 | tf_op jit(solution)/shard_map/ppermute | solution.py:33
  112.2 2.4 %collective-permute-done.17.three_ref = bf16[9,24,128]{2,1,0:T(8,128)(2,1)S(1)} collective-permute-done((bf16[9,24,128]{2,1,0:T(8,128)(2,1)S(1)}, bf16[9,24,128]{2,1,0:T(8,128)(2,1)S(1)}, u32[]{:S(2)}, u32[]{:S(2)}) %collective-permute-start.17) | collective-permute-done | bytes 55328 | tf_op jit(solution)/shard_map/ppermute | solution.py:33
  115.0 1.2 collective-permute-done.18
  116.8 2.1 %collective-permute-start.20 = (bf16[24,256]{1,0:T(8,128)(2,1)S(1)}, bf16[24,256]{1,0:T(8,128)(2,1)S(1)}, u32[]{:S(2)}, u32[]{:S(2)}) collective-permute-start(bf16[24,256]{1,0:T(8,128)(2,1)S(1)} %add.27), channel_id=1, source_target_pairs={{0,4},{2,6},{4,0},{6,2},{1,5},{3,7},{5,1},{7,3},{8,12},{10,14},{12... | collective-permute-start | bytes 36872 | tf_op jit(solution)/shard_map/ppermute | solution.py:33
  118.9 2.1 %collective-permute-start.21 = (bf16[24,256]{1,0:T(8,128)(2,1)S(1)}, bf16[24,256]{1,0:T(8,128)(2,1)S(1)}, u32[]{:S(2)}, u32[]{:S(2)}) collective-permute-start(bf16[24,256]{1,0:T(8,128)(2,1)S(1)} %add.27), channel_id=1, source_target_pairs={{0,6},{2,4},{4,2},{6,0},{1,7},{3,5},{5,3},{7,1},{8,14},{10,12},{12... | collective-permute-start | bytes 36872 | tf_op jit(solution)/shard_map/ppermute | solution.py:33
  122.0 1.8 %collective-permute-done.21 = bf16[24,256]{1,0:T(8,128)(2,1)S(1)} collective-permute-done((bf16[24,256]{1,0:T(8,128)(2,1)S(1)}, bf16[24,256]{1,0:T(8,128)(2,1)S(1)}, u32[]{:S(2)}, u32[]{:S(2)}) %collective-permute-start.21) | collective-permute-done | bytes 12320 | tf_op jit(solution)/shard_map/ppermute | solution.py:33
  (79 shorter events, 10.5 us)
Async XLA Ops:
  26.0 15.1 %copy-start = (bf16[2048,544]{0,1:T(8,128)(2,1)S(1)}, bf16[2048,544]{0,1:T(8,128)(2,1)}, u32[]{:S(2)}) copy-start(bf16[2048,544]{0,1:T(8,128)(2,1)} %param.32) | copy-start | bytes 6684676
  26.0 15.1 %copy-start.7 = (f32[8,3,2048]{2,0,1:T(8,128)S(1)}, f32[8,3,2048]{2,0,1:T(8,128)}, u32[]{:S(2)}) copy-start(f32[8,3,2048]{2,0,1:T(8,128)} %param.50) | copy-start | bytes 589828
  26.0 15.1 %copy-start.11 = (f32[4,2048]{1,0:T(4,128)S(1)}, f32[4,2048]{1,0:T(4,128)}, u32[]{:S(2)}) copy-start(f32[4,2048]{1,0:T(4,128)} %taps_ref.1) | copy-start | bytes 98308
  26.0 15.1 %copy-start.13 = (f32[2048]{0:T(1024)S(1)}, f32[2048]{0:T(1024)}, u32[]{:S(2)}) copy-start(f32[2048]{0:T(1024)} %param.31) | copy-start | bytes 24580
  42.5 11.0 %copy-start.14 = (f32[2048]{0:T(1024)S(1)}, f32[2048]{0:T(1024)}, u32[]{:S(2)}) copy-start(f32[2048]{0:T(1024)} %param.37) | copy-start | bytes 24580
  42.5 11.0 %copy-start.15 = (f32[2048]{0:T(1024)S(1)}, f32[2048]{0:T(1024)}, u32[]{:S(2)}) copy-start(f32[2048]{0:T(1024)} %param.39) | copy-start | bytes 24580
  42.5 11.0 %copy-start.16 = (f32[512]{0:T(512)S(1)}, f32[512]{0:T(512)}, u32[]{:S(2)}) copy-start(f32[512]{0:T(512)} %param.33) | copy-start | bytes 6148
  42.5 11.0 %copy-start.19 = (f32[16]{0:T(128)S(1)}, f32[16]{0:T(128)}, u32[]{:S(2)}) copy-start(f32[16]{0:T(128)} %param.34) | copy-start | bytes 196
  42.5 11.0 %copy-start.20 = (f32[16]{0:T(128)S(1)}, f32[16]{0:T(128)}, u32[]{:S(2)}) copy-start(f32[16]{0:T(128)} %param.35) | copy-start | bytes 196
  42.5 1.3 %collective-permute-start = (bf16[24,544]{1,0:T(8,128)(2,1)S(1)}, bf16[24,544]{1,0:T(8,128)(2,1)S(1)}, u32[]{:S(2)}, u32[]{:S(2)}) collective-permute-start(bf16[24,544]{1,0:T(8,128)(2,1)S(1)} %get-tuple-element.19), channel_id=1, source_target_pairs={{0,1},{1,0},{2,3},{3,2},{4,5},{5,4},{6,7},{7,6},{8,9},{9,8},{10,11... | collective-permute-start | bytes 78344 | tf_op jit(solution)/shard_map/ppermute | solution.py:39
  43.8 5.6 %collective-permute-start.1 = (bf16[24,544]{1,0:T(8,128)(2,1)S(1)}, bf16[24,544]{1,0:T(8,128)(2,1)S(1)}, u32[]{:S(2)}, u32[]{:S(2)}) collective-permute-start(bf16[24,544]{1,0:T(8,128)(2,1)S(1)} %add.24.own_ref), channel_id=1, source_target_pairs={{0,2},{2,0},{4,6},{6,4},{1,3},{3,1},{5,7},{7,5},{8,10},{10,8},{12,... | collective-permute-start | bytes 78344 | tf_op jit(solution)/shard_map/ppermute | solution.py:33
  45.5 5.4 %collective-permute-start.2 = (bf16[24,544]{1,0:T(8,128)(2,1)S(1)}, bf16[24,544]{1,0:T(8,128)(2,1)S(1)}, u32[]{:S(2)}, u32[]{:S(2)}) collective-permute-start(bf16[24,544]{1,0:T(8,128)(2,1)S(1)} %add.24.own_ref), channel_id=1, source_target_pairs={{0,4},{2,6},{4,0},{6,2},{1,5},{3,7},{5,1},{7,3},{8,12},{10,14},{12... | collective-permute-start | bytes 78344 | tf_op jit(solution)/shard_map/ppermute | solution.py:33
  48.4 5.1 %collective-permute-start.3 = (bf16[24,544]{1,0:T(8,128)(2,1)S(1)}, bf16[24,544]{1,0:T(8,128)(2,1)S(1)}, u32[]{:S(2)}, u32[]{:S(2)}) collective-permute-start(bf16[24,544]{1,0:T(8,128)(2,1)S(1)} %add.24.own_ref), channel_id=1, source_target_pairs={{0,6},{2,4},{4,2},{6,0},{1,7},{3,5},{5,3},{7,1},{8,14},{10,12},{12... | collective-permute-start | bytes 78344 | tf_op jit(solution)/shard_map/ppermute | solution.py:33
  63.7 4.8 %collective-permute-start.4 = (bf16[24,1408]{1,0:T(8,128)(2,1)S(1)}, bf16[24,1408]{1,0:T(8,128)(2,1)S(1)}, u32[]{:S(2)}, u32[]{:S(2)}) collective-permute-start(bf16[24,1408]{1,0:T(8,128)(2,1)S(1)} %get-tuple-element.23.refs_0_), channel_id=1, source_target_pairs={{0,8},{8,0},{16,24},{24,16},{1,9},{9,1},{17,25},{25,17},{2,10},{10... | collective-permute-start | bytes 202760 | tf_op jit(solution)/shard_map/ppermute | solution.py:33
  64.3 6.2 %collective-permute-start.5 = (bf16[24,1408]{1,0:T(8,128)(2,1)S(1)}, bf16[24,1408]{1,0:T(8,128)(2,1)S(1)}, u32[]{:S(2)}, u32[]{:S(2)}) collective-permute-start(bf16[24,1408]{1,0:T(8,128)(2,1)S(1)} %get-tuple-element.23.refs_0_), channel_id=1, source_target_pairs={{0,16},{8,24},{16,0},{24,8},{1,17},{9,25},{17,1},{25,9},{2,18},{10... | collective-permute-start | bytes 202760 | tf_op jit(solution)/shard_map/ppermute | solution.py:33
  67.3 5.5 %collective-permute-start.6 = (bf16[24,1408]{1,0:T(8,128)(2,1)S(1)}, bf16[24,1408]{1,0:T(8,128)(2,1)S(1)}, u32[]{:S(2)}, u32[]{:S(2)}) collective-permute-start(bf16[24,1408]{1,0:T(8,128)(2,1)S(1)} %get-tuple-element.23.refs_0_), channel_id=1, source_target_pairs={{0,24},{8,16},{16,8},{24,0},{1,25},{9,17},{17,9},{25,1},{2,26},{10... | collective-permute-start | bytes 202760 | tf_op jit(solution)/shard_map/ppermute | solution.py:33
  72.9 4.6 %collective-permute-start.7 = (bf16[24,1408]{1,0:T(8,128)(2,1)S(1)}, bf16[24,1408]{1,0:T(8,128)(2,1)S(1)}, u32[]{:S(2)}, u32[]{:S(2)}) collective-permute-start(bf16[24,1408]{1,0:T(8,128)(2,1)S(1)} %shard_map.286.refs_0_), channel_id=1, source_target_pairs={{0,32},{32,0},{1,33},{33,1},{2,34},{34,2},{3,35},{35,3},{4,36},{36... | collective-permute-start | bytes 202760 | tf_op jit(solution)/shard_map/ppermute | solution.py:39
  77.7 10.6 %collective-permute-start.10 = (bf16[24,1408]{1,0:T(8,128)(2,1)S(1)}, bf16[24,1408]{1,0:T(8,128)(2,1)S(1)}, u32[]{:S(2)}, u32[]{:S(2)}) collective-permute-start(bf16[24,1408]{1,0:T(8,128)(2,1)S(1)} %shard_map.287.own_ref), channel_id=1, source_target_pairs={{0,192},{64,128},{128,64},{192,0},{1,193},{65,129},{129,65},{193,1... | collective-permute-start | bytes 202760 | tf_op jit(solution)/shard_map/ppermute | solution.py:33
  78.1 10.2 %collective-permute-start.8 = (bf16[24,1408]{1,0:T(8,128)(2,1)S(1)}, bf16[24,1408]{1,0:T(8,128)(2,1)S(1)}, u32[]{:S(2)}, u32[]{:S(2)}) collective-permute-start(bf16[24,1408]{1,0:T(8,128)(2,1)S(1)} %shard_map.287.own_ref), channel_id=1, source_target_pairs={{0,64},{64,0},{128,192},{192,128},{1,65},{65,1},{129,193},{193,129... | collective-permute-start | bytes 202760 | tf_op jit(solution)/shard_map/ppermute | solution.py:33
  79.0 9.3 %collective-permute-start.9 = (bf16[24,1408]{1,0:T(8,128)(2,1)S(1)}, bf16[24,1408]{1,0:T(8,128)(2,1)S(1)}, u32[]{:S(2)}, u32[]{:S(2)}) collective-permute-start(bf16[24,1408]{1,0:T(8,128)(2,1)S(1)} %shard_map.287.own_ref), channel_id=1, source_target_pairs={{0,128},{64,192},{128,0},{192,64},{1,129},{65,193},{129,1},{193,65... | collective-permute-start | bytes 202760 | tf_op jit(solution)/shard_map/ppermute | solution.py:33
  90.2 4.7 %collective-permute-start.11 = (bf16[9,24,128]{2,1,0:T(8,128)(2,1)S(1)}, bf16[9,24,128]{2,1,0:T(8,128)(2,1)S(1)}, u32[]{:S(2)}, u32[]{:S(2)}) collective-permute-start(bf16[9,24,128]{2,1,0:T(8,128)(2,1)S(1)} %get-tuple-element.28.refs_0_), channel_id=1, source_target_pairs={{0,8},{8,0},{16,24},{24,16},{1,9},{9,1},{17,25},{25,17},{2,10},{10... | collective-permute-start | bytes 165896 | tf_op jit(solution)/shard_map/ppermute | solution.py:33
  90.2 5.7 %collective-permute-start.12 = (bf16[9,24,128]{2,1,0:T(8,128)(2,1)S(1)}, bf16[9,24,128]{2,1,0:T(8,128)(2,1)S(1)}, u32[]{:S(2)}, u32[]{:S(2)}) collective-permute-start(bf16[9,24,128]{2,1,0:T(8,128)(2,1)S(1)} %get-tuple-element.28.refs_0_), channel_id=1, source_target_pairs={{0,16},{8,24},{16,0},{24,8},{1,17},{9,25},{17,1},{25,9},{2,18},{10... | collective-permute-start | bytes 165896 | tf_op jit(solution)/shard_map/ppermute | solution.py:33
  92.5 5.4 %collective-permute-start.13 = (bf16[9,24,128]{2,1,0:T(8,128)(2,1)S(1)}, bf16[9,24,128]{2,1,0:T(8,128)(2,1)S(1)}, u32[]{:S(2)}, u32[]{:S(2)}) collective-permute-start(bf16[9,24,128]{2,1,0:T(8,128)(2,1)S(1)} %get-tuple-element.28.refs_0_), channel_id=1, source_target_pairs={{0,24},{8,16},{16,8},{24,0},{1,25},{9,17},{17,9},{25,1},{2,26},{10... | collective-permute-start | bytes 165896 | tf_op jit(solution)/shard_map/ppermute | solution.py:33
  98.2 16.4 %copy-start.6 = (bf16[1024,256]{1,0:T(8,128)(2,1)S(1)}, bf16[1024,256]{1,0:T(8,128)(2,1)}, u32[]{:S(2)}) copy-start(bf16[1024,256]{1,0:T(8,128)(2,1)} %weight_ref.1) | copy-start | bytes 1572868
  98.2 4.2 %collective-permute-start.14 = (bf16[9,24,128]{2,1,0:T(8,128)(2,1)S(1)}, bf16[9,24,128]{2,1,0:T(8,128)(2,1)S(1)}, u32[]{:S(2)}, u32[]{:S(2)}) collective-permute-start(bf16[9,24,128]{2,1,0:T(8,128)(2,1)S(1)} %shard_map.289.refs_0_), channel_id=1, source_target_pairs={{0,32},{32,0},{1,33},{33,1},{2,34},{34,2},{3,35},{35,3},{4,36},{36... | collective-permute-start | bytes 165896 | tf_op jit(solution)/shard_map/ppermute | solution.py:39
  102.7 6.6 %collective-permute-start.15 = (bf16[9,24,128]{2,1,0:T(8,128)(2,1)S(1)}, bf16[9,24,128]{2,1,0:T(8,128)(2,1)S(1)}, u32[]{:S(2)}, u32[]{:S(2)}) collective-permute-start(bf16[9,24,128]{2,1,0:T(8,128)(2,1)S(1)} %shard_map.290.own_ref), channel_id=1, source_target_pairs={{0,64},{64,0},{128,192},{192,128},{1,65},{65,1},{129,193},{193,129... | collective-permute-start | bytes 165896 | tf_op jit(solution)/shard_map/ppermute | solution.py:33
  104.1 8.1 %collective-permute-start.16 = (bf16[9,24,128]{2,1,0:T(8,128)(2,1)S(1)}, bf16[9,24,128]{2,1,0:T(8,128)(2,1)S(1)}, u32[]{:S(2)}, u32[]{:S(2)}) collective-permute-start(bf16[9,24,128]{2,1,0:T(8,128)(2,1)S(1)} %shard_map.290.own_ref), channel_id=1, source_target_pairs={{0,128},{64,192},{128,0},{192,64},{1,129},{65,193},{129,1},{193,65... | collective-permute-start | bytes 165896 | tf_op jit(solution)/shard_map/ppermute | solution.py:33
  108.3 6.3 %collective-permute-start.17 = (bf16[9,24,128]{2,1,0:T(8,128)(2,1)S(1)}, bf16[9,24,128]{2,1,0:T(8,128)(2,1)S(1)}, u32[]{:S(2)}, u32[]{:S(2)}) collective-permute-start(bf16[9,24,128]{2,1,0:T(8,128)(2,1)S(1)} %shard_map.290.own_ref), channel_id=1, source_target_pairs={{0,192},{64,128},{128,64},{192,0},{1,193},{65,129},{129,65},{193,1... | collective-permute-start | bytes 165896 | tf_op jit(solution)/shard_map/ppermute | solution.py:33
  115.0 1.2 collective-permute-start.18
  116.2 4.7 %collective-permute-start.19 = (bf16[24,256]{1,0:T(8,128)(2,1)S(1)}, bf16[24,256]{1,0:T(8,128)(2,1)S(1)}, u32[]{:S(2)}, u32[]{:S(2)}) collective-permute-start(bf16[24,256]{1,0:T(8,128)(2,1)S(1)} %add.27), channel_id=1, source_target_pairs={{0,2},{2,0},{4,6},{6,4},{1,3},{3,1},{5,7},{7,5},{8,10},{10,8},{12,... | collective-permute-start | bytes 36872 | tf_op jit(solution)/shard_map/ppermute | solution.py:33
  116.8 5.2 %collective-permute-start.20 = (bf16[24,256]{1,0:T(8,128)(2,1)S(1)}, bf16[24,256]{1,0:T(8,128)(2,1)S(1)}, u32[]{:S(2)}, u32[]{:S(2)}) collective-permute-start(bf16[24,256]{1,0:T(8,128)(2,1)S(1)} %add.27), channel_id=1, source_target_pairs={{0,4},{2,6},{4,0},{6,2},{1,5},{3,7},{5,1},{7,3},{8,12},{10,14},{12... | collective-permute-start | bytes 36872 | tf_op jit(solution)/shard_map/ppermute | solution.py:33
  118.9 4.9 %collective-permute-start.21 = (bf16[24,256]{1,0:T(8,128)(2,1)S(1)}, bf16[24,256]{1,0:T(8,128)(2,1)S(1)}, u32[]{:S(2)}, u32[]{:S(2)}) collective-permute-start(bf16[24,256]{1,0:T(8,128)(2,1)S(1)} %add.27), channel_id=1, source_target_pairs={{0,6},{2,4},{4,2},{6,0},{1,7},{3,5},{5,3},{7,1},{8,14},{10,12},{12... | collective-permute-start | bytes 36872 | tf_op jit(solution)/shard_map/ppermute | solution.py:33
  (13 other events, 132.4 us)

commit v2 on v1

--- a/solution.py
+++ b/solution.py
@@ -176,33 +176,34 @@
         y = jnp.concatenate(y, axis=0) + skip_ref[:, cols] * mixed[:, cols]
         scanned.append((y * silu(gate_ref[tiles + tile].astype(f32))).astype(bf16))
     total = jnp.dot(jnp.concatenate(scanned, axis=1), op_ref[...], preferred_element_type=f32)
-    part = total.astype(bf16)
-    for target in range(part_ref.shape[0]):
-        part_ref[target] = part
-
-
-def qkv_kernel(parts_ref, rows_ref, gain_ref, wq_ref, wk_ref, wv_ref, residual_ref, out_ref):
-    total = parts_ref[0].astype(f32)
-    for source in range(1, parts_ref.shape[0]):
-        total = total + parts_ref[source].astype(f32)
-    residual = rows_ref[...].astype(f32) + total
+    part_ref[...] = total.astype(bf16)
+
+
+def qkv_kernel(
+    own_ref, one_ref, two_ref, three_ref, rows_ref, gain_ref, wq_ref, wk_ref, wv_ref,
+    residual_ref, out_ref,
+):
+    residual = rows_ref[...].astype(f32) + sum_refs((own_ref, one_ref, two_ref, three_ref))
     residual_ref[...] = residual
     scaled = (residual * gain_ref[...]).astype(bf16)
     column = jnp.sum(residual * residual, axis=1, keepdims=True)
-    at = 0
+    eye = row_index(ALL_ROWS) == lane_index(ALL_ROWS)
+    squares = jnp.sum(jnp.where(eye, column, 0.0), axis=0, keepdims=True)
+    blocks = []
     for weight_ref in (wq_ref, wk_ref, wv_ref):
-        width = weight_ref.shape[1]
-        out_ref[:, at : at + width] = jnp.dot(
-            scaled, weight_ref[...], preferred_element_type=f32
-        ).astype(bf16)
-        at += width
-    out_ref[:, at:] = pair_columns(column).astype(bf16)
-
-
-def pair_columns(column):
-    hi = rounded(column)
-    which = lane_index(ALL_ROWS)
-    return jnp.where(which == 0, hi, jnp.where(which == 1, column - hi, 0.0))
+        part = jnp.dot(scaled, weight_ref[...], preferred_element_type=f32)
+        blocks += [part[:, at : at + HEAD] for at in range(0, part.shape[1], HEAD)]
+    out_ref[...] = jnp.concatenate(blocks + [pair_rows(squares)], axis=0).astype(bf16)
+
+
+def pair_rows(squares):
+    hi = rounded(squares)
+    which = row_index(8)
+    return jnp.where(which == 0, hi, jnp.where(which == 1, squares - hi, 0.0))
+
+
+def pair_total(total):
+    return total[-8:-7] + total[-7:-6]
 
 
 def sum_refs(refs):
@@ -215,9 +216,8 @@
 def qkv_sum_kernel(*refs):
     out_ref = refs[-1]
     total = sum_refs(refs[:-1])
-    column = jnp.sum(total[:, -LANES:], axis=1, keepdims=True)
-    out_ref[:, :-LANES] = total[:, :-LANES].astype(bf16)
-    out_ref[:, -LANES:] = pair_columns(column).astype(bf16)
+    stats = pair_rows(pair_total(total))
+    out_ref[...] = jnp.concatenate([total[:-8], stats], axis=0).astype(bf16)
 
 
 def pack_logs(logs):
@@ -241,12 +241,16 @@
     new_keys_ref, new_values_ref, out_ref, query, fresh_k, fresh_v,
 ):
     total = sum_refs((own_ref, one_ref, two_ref, three_ref))
-    column = jnp.sum(total[:, -LANES:], axis=1, keepdims=True)
-    total = rounded(total[:, :-LANES] * lax.rsqrt(column / width_all + 1e-06))
-    heads = total.shape[1] // HEAD - 2
+    eye = row_index(ALL_ROWS) == lane_index(ALL_ROWS)
+    column = jnp.sum(jnp.where(eye, pair_total(total), 0.0), axis=1, keepdims=True)
+    scale = lax.rsqrt(column / width_all + 1e-06)
+    blocks = [
+        rounded(total[at : at + ALL_ROWS] * scale)
+        for at in range(0, total.shape[0] - 8, ALL_ROWS)
+    ]
+    heads = len(blocks) - 2
     queries = STEPS * heads
-    keys_now = total[:, heads * HEAD : (heads + 1) * HEAD]
-    values_now = total[:, (heads + 1) * HEAD :]
+    keys_now, values_now = blocks[heads:]
     new_keys_ref[...] = keys_now.astype(bf16)
     new_values_ref[...] = values_now.astype(bf16)
     fresh_k[...] = jnp.zeros_like(fresh_k)
@@ -256,9 +260,7 @@
         fresh_k[pl.ds(s, ROWS, stride=8), :] = keys_now[rows]
         fresh_v[pl.ds(s, ROWS, stride=8), :] = values_now[rows]
         for g in range(heads):
-            query[pl.ds(s * heads + g, ROWS, stride=queries), :] = total[
-                rows, g * HEAD : (g + 1) * HEAD
-            ]
+            query[pl.ds(s * heads + g, ROWS, stride=queries), :] = blocks[g][rows]
     which = lane_index(queries, 8)
     fresh_live = (which * heads <= row_index(queries, 8)) & (which < STEPS)
     fresh_live = fresh_live & (first_ref[0] == 1)
@@ -372,7 +374,7 @@
     dt_bias, a_log, d_skip, out_proj, norm_attn, w_query, key_matrix, value_matrix, w_out,
     cache_k, value_cache, lengths, block_of_slot, conv_state, ssm_state,
 ):
-    ctx_size, tp_size = (lax.axis_size(axis) for axis in (CTX, TP))
+    ctx_size = lax.axis_size(CTX)
     local_width = embeds.shape[2]
     width_all = float(local_width * ctx_size)
     channels = in_x.shape[1]
@@ -428,7 +430,7 @@
     state = ssm_state.reshape(ROWS, DS, chunk_count, LANES).transpose(2, 1, 0, 3)
     state, part = call(
         scan_kernel,
-        [(tiled, f32), ((tp_size, ALL_ROWS, local_width), bf16)],
+        [(tiled, f32), ((ALL_ROWS, local_width), bf16)],
         low,
         *from_partners(low, "y"),
         dt_norm.reshape(1, -1),
@@ -449,20 +451,21 @@
         ],
     )
     state = state.transpose(2, 1, 0, 3).reshape(ssm_state.shape)
-    part = exchange(part, TP)
-
-    packed_width = (heads + 3) * HEAD
+    part = over_cores(part)
+
+    packed = ((heads + 2) * ALL_ROWS + 8, HEAD)
     residual, projected = call(
         qkv_kernel,
-        [((ALL_ROWS, local_width), f32), ((ALL_ROWS, packed_width), bf16)],
+        [((ALL_ROWS, local_width), f32), (packed, bf16)],
         part,
+        *from_partners(part, "y"),
         rows_in,
         norm_attn.reshape(1, -1),
         w_query,
         key_matrix,
         value_matrix,
     )
-    shape = ((ALL_ROWS, packed_width), bf16)
+    shape = (packed, bf16)
     (projected,) = call(qkv_sum_kernel, [shape], projected, *from_partners(projected))
     (projected,) = call(qkv_sum_kernel, [shape], projected, from_other(projected, "zb"))
     others = from_partners(projected, "za")

time: 126 us -> 126 us (level); the launches traced: 124 us -> 126 us
  blocking collectives: 45.9 us -> 37.7 us
  starting transfers between devices: 34 us -> 40.4 us
  waiting for transfers between devices: 29.1 us -> 32.4 us
    all_to_all x3 -> x2, blocking collectives: 45.9 us -> 37.7 us  [exchange(): return lax.all_to_all(parts, axis, 0, 0, tiled=True)]
    ppermute x18 -> x21, starting transfers between devices: 32.1 us -> 37.7 us  [from_partners(): lax.ppermute(part, axis, [(i, i ^ flip) for i in range(4)])]
    ppermute x18 -> x21, waiting for transfers between devices: 19.6 us -> 22.8 us  [from_partners(): lax.ppermute(part, axis, [(i, i ^ flip) for i in range(4)])]
    ppermute x4 -> x5, starting transfers between devices: 1.83 us -> 2.66 us  [from_other(): return lax.ppermute(part, axis, [(0, 1), (1, 0)])]
    ppermute x4 -> x5, waiting for transfers between devices: 9.51 us -> 9.59 us  [from_other(): return lax.ppermute(part, axis, [(0, 1), (1, 0)])]
  transfers between devices with their start and end apart: 22 -> 26, of which waited for: 14 -> 18; matrix products, arithmetic and copies ran while one was open for 4% -> 4% of each run, Pallas kernels for 0% -> 0%
where the time goes in v2:
time: 126 us
  starting transfers between devices  40.4 us (32%)
  blocking collectives  37.7 us (30%)
  waiting for transfers between devices  32.4 us (26%)
  Pallas kernels  8.75 us (7%)
  local copies, waits for them, and re-layouts  4.89 us (4%)
    all_to_all x2, blocking collectives, exchange(): return lax.all_to_all(parts, axis, 0, 0, tiled=True)  37.7 us
    ppermute x21, starting transfers between devices, from_partners(): lax.ppermute(part, axis, [(i, i ^ flip) for i in range(4)])  37.7 us
    ppermute x21, waiting for transfers between devices, from_partners(): lax.ppermute(part, axis, [(i, i ^ flip) for i in range(4)])  22.8 us
    ppermute x5, waiting for transfers between devices, from_other(): return lax.ppermute(part, axis, [(0, 1), (1, 0)])  9.59 us
    pallas_call x11, Pallas kernels, call(): pl.pallas_call(kernel, out_shape=[jax.ShapeDtypeStruct(shape, dtype) for...  8.75 us
    ppermute x5, starting transfers between devices, from_other(): return lax.ppermute(part, axis, [(0, 1), (1, 0)])  2.66 us
  transfers between devices with their start and end apart: 26, of which 18 were waited for; matrix products, arithmetic and copies ran while one was open for 4% of the time, Pallas kernels for 0%

profile of v2, /device:TPU:6, one launch (start us, length us, event | category | flops | bytes accessed | tf_op | source)
XLA Modules:
  0.0 125.7 jit_solution(9014190995036052543)
XLA Ops:
  0.6 2.6 %shard_map.281 = bf16[2,16,32,128]{3,2,1,0:T(8,128)(2,1)} custom-call(bf16[24,256]{1,0:T(8,128)(2,1)} %bitcast.33, f32[1,256]{1,0:T(1,128)} %bitcast.46, bf16[256,2048]{1,0:T(8,128)(2,1)} %wx_hbm.1, bf16[256,2048]{1,0:T(8,128)(2,1)} %wz_hbm.1), custom_call_target="tpu_custom_call" | custom-call | flops 3000000000 | bytes 8388608 | tf_op jit(solution)/shard_map/pallas_call | solution.py:47
  3.2 22.8 %all_to_all.10.in_ref = bf16[32,32,128]{2,1,0:T(8,128)(2,1)S(1)} all-to-all(bf16[32,32,128]{2,1,0:T(8,128)(2,1)} %bitcast.45), channel_id=1, replica_groups=mesh['za'=4,'zb'=2,'x'=4,'y'=4,'core'=2] {'za','zb','x'}, dimensions={0} | all-to-all | bytes 524288 | tf_op jit(solution)/shard_map/all_to_all | solution.py:28
  26.2 14.9 %all_to_all.11.inner_ref.gate_ref = bf16[32,24,128]{2,1,0:T(8,128)(2,1)S(1)} all-to-all(bf16[32,24,128]{2,1,0:T(8,128)(2,1)S(1)} %shard_map.282), channel_id=1, replica_groups=mesh['za'=4,'zb'=2,'x'=4,'y'=4,'core'=2] {'za','zb','x'}, dimensions={0} | all-to-all | bytes 393216 | tf_op jit(solution)/shard_map/all_to_all | solution.py:28
  43.8 1.7 %collective-permute-start.1 = (bf16[24,544]{1,0:T(8,128)(2,1)S(1)}, bf16[24,544]{1,0:T(8,128)(2,1)S(1)}, u32[]{:S(2)}, u32[]{:S(2)}) collective-permute-start(bf16[24,544]{1,0:T(8,128)(2,1)S(1)} %add.27.own_ref), channel_id=1, source_target_pairs={{0,2},{2,0},{4,6},{6,4},{1,3},{3,1},{5,7},{7,5},{8,10},{10,8},{12,... | collective-permute-start | bytes 78344 | tf_op jit(solution)/shard_map/ppermute | solution.py:33
  45.5 2.9 %collective-permute-start.2 = (bf16[24,544]{1,0:T(8,128)(2,1)S(1)}, bf16[24,544]{1,0:T(8,128)(2,1)S(1)}, u32[]{:S(2)}, u32[]{:S(2)}) collective-permute-start(bf16[24,544]{1,0:T(8,128)(2,1)S(1)} %add.27.own_ref), channel_id=1, source_target_pairs={{0,4},{2,6},{4,0},{6,2},{1,5},{3,7},{5,1},{7,3},{8,12},{10,14},{12... | collective-permute-start | bytes 78344 | tf_op jit(solution)/shard_map/ppermute | solution.py:33
  49.5 1.5 %collective-permute-done.2.two_ref = bf16[24,544]{1,0:T(8,128)(2,1)S(1)} collective-permute-done((bf16[24,544]{1,0:T(8,128)(2,1)S(1)}, bf16[24,544]{1,0:T(8,128)(2,1)S(1)}, u32[]{:S(2)}, u32[]{:S(2)}) %collective-permute-start.2) | collective-permute-done | bytes 26144 | tf_op jit(solution)/shard_map/ppermute | solution.py:33
  50.9 2.6 %collective-permute-done.3.three_ref = bf16[24,544]{1,0:T(8,128)(2,1)S(1)} collective-permute-done((bf16[24,544]{1,0:T(8,128)(2,1)S(1)}, bf16[24,544]{1,0:T(8,128)(2,1)S(1)}, u32[]{:S(2)}, u32[]{:S(2)}) %collective-permute-start.3) | collective-permute-done | bytes 26144 | tf_op jit(solution)/shard_map/ppermute | solution.py:33
  53.6 1.6 %shard_map.284 = (f32[16,16,8,128]{3,2,1,0:T(8,128)S(1)}, bf16[24,256]{1,0:T(8,128)(2,1)S(1)}) custom-call(bf16[24,544]{1,0:T(8,128)(2,1)S(1)} %add.27.own_ref, bf16[24,544]{1,0:T(8,128)(2,1)S(1)} %collective-permute-done.1.one_ref, bf16[24,544]{1,0:T(8,128)(2,1)S(1)} %collective-permute-done.2.two_ref, ...), custom_call_target="tpu_custom_call" | custom-call | flops 3000000000 | bytes 8388608 | tf_op jit(solution)/shard_map/pallas_call | solution.py:47
  56.4 1.7 %collective-permute-start.6 = (bf16[24,256]{1,0:T(8,128)(2,1)S(1)}, bf16[24,256]{1,0:T(8,128)(2,1)S(1)}, u32[]{:S(2)}, u32[]{:S(2)}) collective-permute-start(bf16[24,256]{1,0:T(8,128)(2,1)S(1)} %add.28.own_ref), channel_id=1, source_target_pairs={{0,4},{2,6},{4,0},{6,2},{1,5},{3,7},{5,1},{7,3},{8,12},{10,14},{12... | collective-permute-start | bytes 36872 | tf_op jit(solution)/shard_map/ppermute | solution.py:33
  58.1 3.0 %collective-permute-start.7 = (bf16[24,256]{1,0:T(8,128)(2,1)S(1)}, bf16[24,256]{1,0:T(8,128)(2,1)S(1)}, u32[]{:S(2)}, u32[]{:S(2)}) collective-permute-start(bf16[24,256]{1,0:T(8,128)(2,1)S(1)} %add.28.own_ref), channel_id=1, source_target_pairs={{0,6},{2,4},{4,2},{6,0},{1,7},{3,5},{5,3},{7,1},{8,14},{10,12},{12... | collective-permute-start | bytes 36872 | tf_op jit(solution)/shard_map/ppermute | solution.py:33
  63.2 2.1 %collective-permute-start.10 = (bf16[248,128]{1,0:T(8,128)(2,1)S(1)}, bf16[248,128]{1,0:T(8,128)(2,1)S(1)}, u32[]{:S(2)}, u32[]{:S(2)}) collective-permute-start(bf16[248,128]{1,0:T(8,128)(2,1)S(1)} %get-tuple-element.23.refs_0_), channel_id=1, source_target_pairs={{0,24},{8,16},{16,8},{24,0},{1,25},{9,17},{17,9},{25,1},{2,26},{10... | collective-permute-start | bytes 190472 | tf_op jit(solution)/shard_map/ppermute | solution.py:33
  65.4 2.6 %collective-permute-start.9 = (bf16[248,128]{1,0:T(8,128)(2,1)S(1)}, bf16[248,128]{1,0:T(8,128)(2,1)S(1)}, u32[]{:S(2)}, u32[]{:S(2)}) collective-permute-start(bf16[248,128]{1,0:T(8,128)(2,1)S(1)} %get-tuple-element.23.refs_0_), channel_id=1, source_target_pairs={{0,16},{8,24},{16,0},{24,8},{1,17},{9,25},{17,1},{25,9},{2,18},{10... | collective-permute-start | bytes 190472 | tf_op jit(solution)/shard_map/ppermute | solution.py:33
  68.0 1.4 %collective-permute-done.10.refs_3_ = bf16[248,128]{1,0:T(8,128)(2,1)S(1)} collective-permute-done((bf16[248,128]{1,0:T(8,128)(2,1)S(1)}, bf16[248,128]{1,0:T(8,128)(2,1)S(1)}, u32[]{:S(2)}, u32[]{:S(2)}) %collective-permute-start.10) | collective-permute-done | bytes 63520 | tf_op jit(solution)/shard_map/ppermute | solution.py:33
  69.6 1.5 %collective-permute-done.9.refs_2_ = bf16[248,128]{1,0:T(8,128)(2,1)S(1)} collective-permute-done((bf16[248,128]{1,0:T(8,128)(2,1)S(1)}, bf16[248,128]{1,0:T(8,128)(2,1)S(1)}, u32[]{:S(2)}, u32[]{:S(2)}) %collective-permute-start.9) | collective-permute-done | bytes 63520 | tf_op jit(solution)/shard_map/ppermute | solution.py:33
  71.9 3.6 %collective-permute-done.11.refs_1_ = bf16[248,128]{1,0:T(8,128)(2,1)S(1)} collective-permute-done((bf16[248,128]{1,0:T(8,128)(2,1)S(1)}, bf16[248,128]{1,0:T(8,128)(2,1)S(1)}, u32[]{:S(2)}, u32[]{:S(2)}) %collective-permute-start.11) | collective-permute-done | bytes 63520 | tf_op jit(solution)/shard_map/ppermute | solution.py:39
  76.7 2.3 %collective-permute-start.13 = (bf16[248,128]{1,0:T(8,128)(2,1)S(1)}, bf16[248,128]{1,0:T(8,128)(2,1)S(1)}, u32[]{:S(2)}, u32[]{:S(2)}) collective-permute-start(bf16[248,128]{1,0:T(8,128)(2,1)S(1)} %shard_map.287.own_ref), channel_id=1, source_target_pairs={{0,128},{64,192},{128,0},{192,64},{1,129},{65,193},{129,1},{193,65... | collective-permute-start | bytes 190472 | tf_op jit(solution)/shard_map/ppermute | solution.py:33
  79.0 3.2 %collective-permute-start.14 = (bf16[248,128]{1,0:T(8,128)(2,1)S(1)}, bf16[248,128]{1,0:T(8,128)(2,1)S(1)}, u32[]{:S(2)}, u32[]{:S(2)}) collective-permute-start(bf16[248,128]{1,0:T(8,128)(2,1)S(1)} %shard_map.287.own_ref), channel_id=1, source_target_pairs={{0,192},{64,128},{128,64},{192,0},{1,193},{65,129},{129,65},{193,1... | collective-permute-start | bytes 190472 | tf_op jit(solution)/shard_map/ppermute | solution.py:33
  82.2 1.6 %copy.32 = f32[8,16,16,128]{3,2,1,0:T(8,128)} copy(f32[8,16,16,128]{3,0,1,2:T(8,128)S(1)} %bitcast.29) | data formatting | bytes 2097152 | tf_op jit(solution)/shard_map/transpose | solution.py:453
  83.8 2.4 %reshape.73 = f32[8,16,2048]{2,1,0:T(8,128)} reshape(f32[8,16,16,128]{3,2,1,0:T(8,128)} %copy.32) | data formatting | bytes 2097152 | tf_op jit(solution)/shard_map/reshape | solution.py:453
  86.2 1.9 %shard_map.288 = (bf16[24,128]{1,0:T(8,128)(2,1)}, bf16[24,128]{1,0:T(8,128)(2,1)}, bf16[9,24,128]{2,1,0:T(8,128)(2,1)S(1)}) custom-call(s32[1]{0:T(128)} %bitcast.13.first_ref, s32[8]{0:T(128)S(1)} %copy-done.21, s32[4,8]{1,0:T(4,128)S(1)} %bitcast.39, bf16[248,128]{1,0:T(8,128)(2,1)S(1)} %shard_map.287.own_ref, ...), custom_call_target="tpu_custom_call" | custom-call | flops 3000000000 | bytes 8388608 | tf_op jit(solution)/shard_map/pallas_call | solution.py:47
  88.0 2.5 %collective-permute-start.15 = (bf16[9,24,128]{2,1,0:T(8,128)(2,1)S(1)}, bf16[9,24,128]{2,1,0:T(8,128)(2,1)S(1)}, u32[]{:S(2)}, u32[]{:S(2)}) collective-permute-start(bf16[9,24,128]{2,1,0:T(8,128)(2,1)S(1)} %get-tuple-element.28.refs_0_), channel_id=1, source_target_pairs={{0,8},{8,0},{16,24},{24,16},{1,9},{9,1},{17,25},{25,17},{2,10},{10... | collective-permute-start | bytes 165896 | tf_op jit(solution)/shard_map/ppermute | solution.py:33
  91.4 1.9 %collective-permute-start.17 = (bf16[9,24,128]{2,1,0:T(8,128)(2,1)S(1)}, bf16[9,24,128]{2,1,0:T(8,128)(2,1)S(1)}, u32[]{:S(2)}, u32[]{:S(2)}) collective-permute-start(bf16[9,24,128]{2,1,0:T(8,128)(2,1)S(1)} %get-tuple-element.28.refs_0_), channel_id=1, source_target_pairs={{0,24},{8,16},{16,8},{24,0},{1,25},{9,17},{17,9},{25,1},{2,26},{10... | collective-permute-start | bytes 165896 | tf_op jit(solution)/shard_map/ppermute | solution.py:33
  93.2 3.0 %collective-permute-done.16.refs_2_ = bf16[9,24,128]{2,1,0:T(8,128)(2,1)S(1)} collective-permute-done((bf16[9,24,128]{2,1,0:T(8,128)(2,1)S(1)}, bf16[9,24,128]{2,1,0:T(8,128)(2,1)S(1)}, u32[]{:S(2)}, u32[]{:S(2)}) %collective-permute-start.16) | collective-permute-done | bytes 55328 | tf_op jit(solution)/shard_map/ppermute | solution.py:33
  97.1 1.8 %collective-permute-start.18 = (bf16[9,24,128]{2,1,0:T(8,128)(2,1)S(1)}, bf16[9,24,128]{2,1,0:T(8,128)(2,1)S(1)}, u32[]{:S(2)}, u32[]{:S(2)}) collective-permute-start(bf16[9,24,128]{2,1,0:T(8,128)(2,1)S(1)} %shard_map.289.refs_0_), channel_id=1, source_target_pairs={{0,32},{32,0},{1,33},{33,1},{2,34},{34,2},{3,35},{35,3},{4,36},{36... | collective-permute-start | bytes 165896 | tf_op jit(solution)/shard_map/ppermute | solution.py:39
  98.9 2.4 %collective-permute-done.18.refs_1_ = bf16[9,24,128]{2,1,0:T(8,128)(2,1)S(1)} collective-permute-done((bf16[9,24,128]{2,1,0:T(8,128)(2,1)S(1)}, bf16[9,24,128]{2,1,0:T(8,128)(2,1)S(1)}, u32[]{:S(2)}, u32[]{:S(2)}) %collective-permute-start.18) | collective-permute-done | bytes 55328 | tf_op jit(solution)/shard_map/ppermute | solution.py:39
  101.6 1.9 %collective-permute-start.19 = (bf16[9,24,128]{2,1,0:T(8,128)(2,1)S(1)}, bf16[9,24,128]{2,1,0:T(8,128)(2,1)S(1)}, u32[]{:S(2)}, u32[]{:S(2)}) collective-permute-start(bf16[9,24,128]{2,1,0:T(8,128)(2,1)S(1)} %shard_map.290.own_ref), channel_id=1, source_target_pairs={{0,64},{64,0},{128,192},{192,128},{1,65},{65,1},{129,193},{193,129... | collective-permute-start | bytes 165896 | tf_op jit(solution)/shard_map/ppermute | solution.py:33
  103.4 3.7 %collective-permute-start.20 = (bf16[9,24,128]{2,1,0:T(8,128)(2,1)S(1)}, bf16[9,24,128]{2,1,0:T(8,128)(2,1)S(1)}, u32[]{:S(2)}, u32[]{:S(2)}) collective-permute-start(bf16[9,24,128]{2,1,0:T(8,128)(2,1)S(1)} %shard_map.290.own_ref), channel_id=1, source_target_pairs={{0,128},{64,192},{128,0},{192,64},{1,129},{65,193},{129,1},{193,65... | collective-permute-start | bytes 165896 | tf_op jit(solution)/shard_map/ppermute | solution.py:33
  108.2 3.3 %collective-permute-done.20.two_ref = bf16[9,24,128]{2,1,0:T(8,128)(2,1)S(1)} collective-permute-done((bf16[9,24,128]{2,1,0:T(8,128)(2,1)S(1)}, bf16[9,24,128]{2,1,0:T(8,128)(2,1)S(1)}, u32[]{:S(2)}, u32[]{:S(2)}) %collective-permute-start.20) | collective-permute-done | bytes 55328 | tf_op jit(solution)/shard_map/ppermute | solution.py:33
  111.5 1.9 %collective-permute-done.21.three_ref = bf16[9,24,128]{2,1,0:T(8,128)(2,1)S(1)} collective-permute-done((bf16[9,24,128]{2,1,0:T(8,128)(2,1)S(1)}, bf16[9,24,128]{2,1,0:T(8,128)(2,1)S(1)}, u32[]{:S(2)}, u32[]{:S(2)}) %collective-permute-start.21) | collective-permute-done | bytes 55328 | tf_op jit(solution)/shard_map/ppermute | solution.py:33
  115.8 4.4 %collective-permute-start.24 = (bf16[24,256]{1,0:T(8,128)(2,1)S(1)}, bf16[24,256]{1,0:T(8,128)(2,1)S(1)}, u32[]{:S(2)}, u32[]{:S(2)}) collective-permute-start(bf16[24,256]{1,0:T(8,128)(2,1)S(1)} %add.31), channel_id=1, source_target_pairs={{0,4},{2,6},{4,0},{6,2},{1,5},{3,7},{5,1},{7,3},{8,12},{10,14},{12... | collective-permute-start | bytes 36872 | tf_op jit(solution)/shard_map/ppermute | solution.py:33
  120.2 1.8 %collective-permute-done.24 = bf16[24,256]{1,0:T(8,128)(2,1)S(1)} collective-permute-done((bf16[24,256]{1,0:T(8,128)(2,1)S(1)}, bf16[24,256]{1,0:T(8,128)(2,1)S(1)}, u32[]{:S(2)}, u32[]{:S(2)}) %collective-permute-start.24) | collective-permute-done | bytes 12320 | tf_op jit(solution)/shard_map/ppermute | solution.py:33
  122.0 3.1 %collective-permute-done.25 = bf16[24,256]{1,0:T(8,128)(2,1)S(1)} collective-permute-done((bf16[24,256]{1,0:T(8,128)(2,1)S(1)}, bf16[24,256]{1,0:T(8,128)(2,1)S(1)}, u32[]{:S(2)}, u32[]{:S(2)}) %collective-permute-start.25) | collective-permute-done | bytes 12320 | tf_op jit(solution)/shard_map/ppermute | solution.py:33
  (87 shorter events, 15.3 us)
Async XLA Ops:
  26.0 15.1 %copy-start = (bf16[2048,544]{0,1:T(8,128)(2,1)S(1)}, bf16[2048,544]{0,1:T(8,128)(2,1)}, u32[]{:S(2)}) copy-start(bf16[2048,544]{0,1:T(8,128)(2,1)} %param.32) | copy-start | bytes 6684676
  26.0 15.1 %copy-start.7 = (f32[8,3,2048]{2,0,1:T(8,128)S(1)}, f32[8,3,2048]{2,0,1:T(8,128)}, u32[]{:S(2)}) copy-start(f32[8,3,2048]{2,0,1:T(8,128)} %param.50) | copy-start | bytes 589828
  26.0 15.1 %copy-start.11 = (f32[4,2048]{1,0:T(4,128)S(1)}, f32[4,2048]{1,0:T(4,128)}, u32[]{:S(2)}) copy-start(f32[4,2048]{1,0:T(4,128)} %taps_ref.1) | copy-start | bytes 98308
  26.0 15.1 %copy-start.13 = (f32[2048]{0:T(1024)S(1)}, f32[2048]{0:T(1024)}, u32[]{:S(2)}) copy-start(f32[2048]{0:T(1024)} %param.31) | copy-start | bytes 24580
  42.5 11.0 %copy-start.15 = (f32[2048]{0:T(1024)S(1)}, f32[2048]{0:T(1024)}, u32[]{:S(2)}) copy-start(f32[2048]{0:T(1024)} %param.39) | copy-start | bytes 24580
  42.5 1.3 %collective-permute-start = (bf16[24,544]{1,0:T(8,128)(2,1)S(1)}, bf16[24,544]{1,0:T(8,128)(2,1)S(1)}, u32[]{:S(2)}, u32[]{:S(2)}) collective-permute-start(bf16[24,544]{1,0:T(8,128)(2,1)S(1)} %get-tuple-element.19), channel_id=1, source_target_pairs={{0,1},{1,0},{2,3},{3,2},{4,5},{5,4},{6,7},{7,6},{8,9},{9,8},{10,11... | collective-permute-start | bytes 78344 | tf_op jit(solution)/shard_map/ppermute | solution.py:39
  43.8 5.6 %collective-permute-start.1 = (bf16[24,544]{1,0:T(8,128)(2,1)S(1)}, bf16[24,544]{1,0:T(8,128)(2,1)S(1)}, u32[]{:S(2)}, u32[]{:S(2)}) collective-permute-start(bf16[24,544]{1,0:T(8,128)(2,1)S(1)} %add.27.own_ref), channel_id=1, source_target_pairs={{0,2},{2,0},{4,6},{6,4},{1,3},{3,1},{5,7},{7,5},{8,10},{10,8},{12,... | collective-permute-start | bytes 78344 | tf_op jit(solution)/shard_map/ppermute | solution.py:33
  45.5 5.4 %collective-permute-start.2 = (bf16[24,544]{1,0:T(8,128)(2,1)S(1)}, bf16[24,544]{1,0:T(8,128)(2,1)S(1)}, u32[]{:S(2)}, u32[]{:S(2)}) collective-permute-start(bf16[24,544]{1,0:T(8,128)(2,1)S(1)} %add.27.own_ref), channel_id=1, source_target_pairs={{0,4},{2,6},{4,0},{6,2},{1,5},{3,7},{5,1},{7,3},{8,12},{10,14},{12... | collective-permute-start | bytes 78344 | tf_op jit(solution)/shard_map/ppermute | solution.py:33
  48.4 5.1 %collective-permute-start.3 = (bf16[24,544]{1,0:T(8,128)(2,1)S(1)}, bf16[24,544]{1,0:T(8,128)(2,1)S(1)}, u32[]{:S(2)}, u32[]{:S(2)}) collective-permute-start(bf16[24,544]{1,0:T(8,128)(2,1)S(1)} %add.27.own_ref), channel_id=1, source_target_pairs={{0,6},{2,4},{4,2},{6,0},{1,7},{3,5},{5,3},{7,1},{8,14},{10,12},{12... | collective-permute-start | bytes 78344 | tf_op jit(solution)/shard_map/ppermute | solution.py:33
  55.2 1.2 collective-permute-start.4
  56.4 4.7 %collective-permute-start.5 = (bf16[24,256]{1,0:T(8,128)(2,1)S(1)}, bf16[24,256]{1,0:T(8,128)(2,1)S(1)}, u32[]{:S(2)}, u32[]{:S(2)}) collective-permute-start(bf16[24,256]{1,0:T(8,128)(2,1)S(1)} %add.28.own_ref), channel_id=1, source_target_pairs={{0,2},{2,0},{4,6},{6,4},{1,3},{3,1},{5,7},{7,5},{8,10},{10,8},{12,... | collective-permute-start | bytes 36872 | tf_op jit(solution)/shard_map/ppermute | solution.py:33
  56.4 5.4 %collective-permute-start.6 = (bf16[24,256]{1,0:T(8,128)(2,1)S(1)}, bf16[24,256]{1,0:T(8,128)(2,1)S(1)}, u32[]{:S(2)}, u32[]{:S(2)}) collective-permute-start(bf16[24,256]{1,0:T(8,128)(2,1)S(1)} %add.28.own_ref), channel_id=1, source_target_pairs={{0,4},{2,6},{4,0},{6,2},{1,5},{3,7},{5,1},{7,3},{8,12},{10,14},{12... | collective-permute-start | bytes 36872 | tf_op jit(solution)/shard_map/ppermute | solution.py:33
  58.1 4.9 %collective-permute-start.7 = (bf16[24,256]{1,0:T(8,128)(2,1)S(1)}, bf16[24,256]{1,0:T(8,128)(2,1)S(1)}, u32[]{:S(2)}, u32[]{:S(2)}) collective-permute-start(bf16[24,256]{1,0:T(8,128)(2,1)S(1)} %add.28.own_ref), channel_id=1, source_target_pairs={{0,6},{2,4},{4,2},{6,0},{1,7},{3,5},{5,3},{7,1},{8,14},{10,12},{12... | collective-permute-start | bytes 36872 | tf_op jit(solution)/shard_map/ppermute | solution.py:33
  63.2 6.1 %collective-permute-start.10 = (bf16[248,128]{1,0:T(8,128)(2,1)S(1)}, bf16[248,128]{1,0:T(8,128)(2,1)S(1)}, u32[]{:S(2)}, u32[]{:S(2)}) collective-permute-start(bf16[248,128]{1,0:T(8,128)(2,1)S(1)} %get-tuple-element.23.refs_0_), channel_id=1, source_target_pairs={{0,24},{8,16},{16,8},{24,0},{1,25},{9,17},{17,9},{25,1},{2,26},{10... | collective-permute-start | bytes 190472 | tf_op jit(solution)/shard_map/ppermute | solution.py:33
  65.4 4.2 %collective-permute-start.8 = (bf16[248,128]{1,0:T(8,128)(2,1)S(1)}, bf16[248,128]{1,0:T(8,128)(2,1)S(1)}, u32[]{:S(2)}, u32[]{:S(2)}) collective-permute-start(bf16[248,128]{1,0:T(8,128)(2,1)S(1)} %get-tuple-element.23.refs_0_), channel_id=1, source_target_pairs={{0,8},{8,0},{16,24},{24,16},{1,9},{9,1},{17,25},{25,17},{2,10},{10... | collective-permute-start | bytes 190472 | tf_op jit(solution)/shard_map/ppermute | solution.py:33
  65.4 5.7 %collective-permute-start.9 = (bf16[248,128]{1,0:T(8,128)(2,1)S(1)}, bf16[248,128]{1,0:T(8,128)(2,1)S(1)}, u32[]{:S(2)}, u32[]{:S(2)}) collective-permute-start(bf16[248,128]{1,0:T(8,128)(2,1)S(1)} %get-tuple-element.23.refs_0_), channel_id=1, source_target_pairs={{0,16},{8,24},{16,0},{24,8},{1,17},{9,25},{17,1},{25,9},{2,18},{10... | collective-permute-start | bytes 190472 | tf_op jit(solution)/shard_map/ppermute | solution.py:33
  71.2 4.3 %collective-permute-start.11 = (bf16[248,128]{1,0:T(8,128)(2,1)S(1)}, bf16[248,128]{1,0:T(8,128)(2,1)S(1)}, u32[]{:S(2)}, u32[]{:S(2)}) collective-permute-start(bf16[248,128]{1,0:T(8,128)(2,1)S(1)} %shard_map.286.refs_0_), channel_id=1, source_target_pairs={{0,32},{32,0},{1,33},{33,1},{2,34},{34,2},{3,35},{35,3},{4,36},{36... | collective-permute-start | bytes 190472 | tf_op jit(solution)/shard_map/ppermute | solution.py:39
  75.6 10.6 %collective-permute-start.12 = (bf16[248,128]{1,0:T(8,128)(2,1)S(1)}, bf16[248,128]{1,0:T(8,128)(2,1)S(1)}, u32[]{:S(2)}, u32[]{:S(2)}) collective-permute-start(bf16[248,128]{1,0:T(8,128)(2,1)S(1)} %shard_map.287.own_ref), channel_id=1, source_target_pairs={{0,64},{64,0},{128,192},{192,128},{1,65},{65,1},{129,193},{193,129... | collective-permute-start | bytes 190472 | tf_op jit(solution)/shard_map/ppermute | solution.py:33
  76.7 9.5 %collective-permute-start.13 = (bf16[248,128]{1,0:T(8,128)(2,1)S(1)}, bf16[248,128]{1,0:T(8,128)(2,1)S(1)}, u32[]{:S(2)}, u32[]{:S(2)}) collective-permute-start(bf16[248,128]{1,0:T(8,128)(2,1)S(1)} %shard_map.287.own_ref), channel_id=1, source_target_pairs={{0,128},{64,192},{128,0},{192,64},{1,129},{65,193},{129,1},{193,65... | collective-permute-start | bytes 190472 | tf_op jit(solution)/shard_map/ppermute | solution.py:33
  79.0 7.2 %collective-permute-start.14 = (bf16[248,128]{1,0:T(8,128)(2,1)S(1)}, bf16[248,128]{1,0:T(8,128)(2,1)S(1)}, u32[]{:S(2)}, u32[]{:S(2)}) collective-permute-start(bf16[248,128]{1,0:T(8,128)(2,1)S(1)} %shard_map.287.own_ref), channel_id=1, source_target_pairs={{0,192},{64,128},{128,64},{192,0},{1,193},{65,129},{129,65},{193,1... | collective-permute-start | bytes 190472 | tf_op jit(solution)/shard_map/ppermute | solution.py:33
  88.0 5.2 %collective-permute-start.15 = (bf16[9,24,128]{2,1,0:T(8,128)(2,1)S(1)}, bf16[9,24,128]{2,1,0:T(8,128)(2,1)S(1)}, u32[]{:S(2)}, u32[]{:S(2)}) collective-permute-start(bf16[9,24,128]{2,1,0:T(8,128)(2,1)S(1)} %get-tuple-element.28.refs_0_), channel_id=1, source_target_pairs={{0,8},{8,0},{16,24},{24,16},{1,9},{9,1},{17,25},{25,17},{2,10},{10... | collective-permute-start | bytes 165896 | tf_op jit(solution)/shard_map/ppermute | solution.py:33
  90.5 5.7 %collective-permute-start.16 = (bf16[9,24,128]{2,1,0:T(8,128)(2,1)S(1)}, bf16[9,24,128]{2,1,0:T(8,128)(2,1)S(1)}, u32[]{:S(2)}, u32[]{:S(2)}) collective-permute-start(bf16[9,24,128]{2,1,0:T(8,128)(2,1)S(1)} %get-tuple-element.28.refs_0_), channel_id=1, source_target_pairs={{0,16},{8,24},{16,0},{24,8},{1,17},{9,25},{17,1},{25,9},{2,18},{10... | collective-permute-start | bytes 165896 | tf_op jit(solution)/shard_map/ppermute | solution.py:33
  91.4 5.4 %collective-permute-start.17 = (bf16[9,24,128]{2,1,0:T(8,128)(2,1)S(1)}, bf16[9,24,128]{2,1,0:T(8,128)(2,1)S(1)}, u32[]{:S(2)}, u32[]{:S(2)}) collective-permute-start(bf16[9,24,128]{2,1,0:T(8,128)(2,1)S(1)} %get-tuple-element.28.refs_0_), channel_id=1, source_target_pairs={{0,24},{8,16},{16,8},{24,0},{1,25},{9,17},{17,9},{25,1},{2,26},{10... | collective-permute-start | bytes 165896 | tf_op jit(solution)/shard_map/ppermute | solution.py:33
  97.1 16.3 %copy-start.6 = (bf16[1024,256]{1,0:T(8,128)(2,1)S(1)}, bf16[1024,256]{1,0:T(8,128)(2,1)}, u32[]{:S(2)}) copy-start(bf16[1024,256]{1,0:T(8,128)(2,1)} %weight_ref.1) | copy-start | bytes 1572868
  97.1 4.2 %collective-permute-start.18 = (bf16[9,24,128]{2,1,0:T(8,128)(2,1)S(1)}, bf16[9,24,128]{2,1,0:T(8,128)(2,1)S(1)}, u32[]{:S(2)}, u32[]{:S(2)}) collective-permute-start(bf16[9,24,128]{2,1,0:T(8,128)(2,1)S(1)} %shard_map.289.refs_0_), channel_id=1, source_target_pairs={{0,32},{32,0},{1,33},{33,1},{2,34},{34,2},{3,35},{35,3},{4,36},{36... | collective-permute-start | bytes 165896 | tf_op jit(solution)/shard_map/ppermute | solution.py:39
  101.6 6.6 %collective-permute-start.19 = (bf16[9,24,128]{2,1,0:T(8,128)(2,1)S(1)}, bf16[9,24,128]{2,1,0:T(8,128)(2,1)S(1)}, u32[]{:S(2)}, u32[]{:S(2)}) collective-permute-start(bf16[9,24,128]{2,1,0:T(8,128)(2,1)S(1)} %shard_map.290.own_ref), channel_id=1, source_target_pairs={{0,64},{64,0},{128,192},{192,128},{1,65},{65,1},{129,193},{193,129... | collective-permute-start | bytes 165896 | tf_op jit(solution)/shard_map/ppermute | solution.py:33
  103.4 8.1 %collective-permute-start.20 = (bf16[9,24,128]{2,1,0:T(8,128)(2,1)S(1)}, bf16[9,24,128]{2,1,0:T(8,128)(2,1)S(1)}, u32[]{:S(2)}, u32[]{:S(2)}) collective-permute-start(bf16[9,24,128]{2,1,0:T(8,128)(2,1)S(1)} %shard_map.290.own_ref), channel_id=1, source_target_pairs={{0,128},{64,192},{128,0},{192,64},{1,129},{65,193},{129,1},{193,65... | collective-permute-start | bytes 165896 | tf_op jit(solution)/shard_map/ppermute | solution.py:33
  107.1 6.3 %collective-permute-start.21 = (bf16[9,24,128]{2,1,0:T(8,128)(2,1)S(1)}, bf16[9,24,128]{2,1,0:T(8,128)(2,1)S(1)}, u32[]{:S(2)}, u32[]{:S(2)}) collective-permute-start(bf16[9,24,128]{2,1,0:T(8,128)(2,1)S(1)} %shard_map.290.own_ref), channel_id=1, source_target_pairs={{0,192},{64,128},{128,64},{192,0},{1,193},{65,129},{129,65},{193,1... | collective-permute-start | bytes 165896 | tf_op jit(solution)/shard_map/ppermute | solution.py:33
  113.9 1.2 collective-permute-start.22
  115.1 5.1 %collective-permute-start.23 = (bf16[24,256]{1,0:T(8,128)(2,1)S(1)}, bf16[24,256]{1,0:T(8,128)(2,1)S(1)}, u32[]{:S(2)}, u32[]{:S(2)}) collective-permute-start(bf16[24,256]{1,0:T(8,128)(2,1)S(1)} %add.31), channel_id=1, source_target_pairs={{0,2},{2,0},{4,6},{6,4},{1,3},{3,1},{5,7},{7,5},{8,10},{10,8},{12,... | collective-permute-start | bytes 36872 | tf_op jit(solution)/shard_map/ppermute | solution.py:33
  115.8 6.2 %collective-permute-start.24 = (bf16[24,256]{1,0:T(8,128)(2,1)S(1)}, bf16[24,256]{1,0:T(8,128)(2,1)S(1)}, u32[]{:S(2)}, u32[]{:S(2)}) collective-permute-start(bf16[24,256]{1,0:T(8,128)(2,1)S(1)} %add.31), channel_id=1, source_target_pairs={{0,4},{2,6},{4,0},{6,2},{1,5},{3,7},{5,1},{7,3},{8,12},{10,14},{12... | collective-permute-start | bytes 36872 | tf_op jit(solution)/shard_map/ppermute | solution.py:33
  120.2 4.9 %collective-permute-start.25 = (bf16[24,256]{1,0:T(8,128)(2,1)S(1)}, bf16[24,256]{1,0:T(8,128)(2,1)S(1)}, u32[]{:S(2)}, u32[]{:S(2)}) collective-permute-start(bf16[24,256]{1,0:T(8,128)(2,1)S(1)} %add.31), channel_id=1, source_target_pairs={{0,6},{2,4},{4,2},{6,0},{1,7},{3,5},{5,3},{7,1},{8,14},{10,12},{12... | collective-permute-start | bytes 36872 | tf_op jit(solution)/shard_map/ppermute | solution.py:33
  (17 other events, 174.2 us)

commit v3 on v2

--- a/solution.py
+++ b/solution.py
@@ -221,18 +221,15 @@
 
 
 def pack_logs(logs):
-    which = lane_index(ALL_ROWS)
-    logs = jnp.where(which < ROWS, logs, 0.0)
+    logs = jnp.where(lane_index(ROWS) < 32, logs, 0.0)
     hi = rounded(logs)
     mid = rounded(logs - hi)
     low = logs - hi - mid
-    return hi + pltpu.roll(mid, ROWS, 1) + pltpu.roll(low, 2 * ROWS, 1)
+    return hi + pltpu.roll(mid, 32, 1) + pltpu.roll(low, 64, 1)
 
 
 def unpack_logs(packed):
-    return (
-        packed + pltpu.roll(packed, LANES - ROWS, 1) + pltpu.roll(packed, LANES - 2 * ROWS, 1)
-    )
+    return packed + pltpu.roll(packed, LANES - 32, 1) + pltpu.roll(packed, LANES - 64, 1)
 
 
 def attention_kernel(
@@ -314,43 +311,47 @@
         jnp.sum(weights[b], axis=1, keepdims=True) + jnp.sum(fresh[b], axis=1, keepdims=True)
         for b in every
     ]
-    logs = jnp.zeros((queries, LANES), f32)
+    eye = lanes == row_index(queries)
+    blocks, logs = [], []
     for b in every:
         any_live = sums[b] > 0
         safe = jnp.where(any_live, sums[b], 1.0)
-        out_ref[b] = (attended[b] / safe).astype(bf16)
+        blocks.append(attended[b] / safe)
         log_sum = jnp.where(any_live, peaks[b] + jnp.log(safe), NEGATIVE)
-        logs = jnp.where(lanes == b, log_sum, logs)
-    out_ref[ROWS] = pack_logs(logs).astype(bf16)
-
-
-def shares_of(refs):
-    logs = [unpack_logs(ref[ROWS].astype(f32)) for ref in refs]
+        logs.append(jnp.sum(jnp.where(eye, log_sum, 0.0), axis=0, keepdims=True))
+    blocks.append(pack_logs(jnp.concatenate(logs, axis=0)))
+    out_ref[...] = jnp.concatenate(blocks, axis=0).astype(bf16)
+
+
+def combined(refs):
+    parts = [ref[...].astype(f32) for ref in refs]
+    logs = [unpack_logs(part[-ROWS:]) for part in parts]
     top = functools.reduce(jnp.maximum, logs)
     shares = [jnp.exp(log - top) for log in logs]
     total = functools.reduce(jnp.add, shares)
-    return [share / total for share in shares], top + jnp.log(total)
-
-
-def combined_row(refs, shares, b):
-    attended = [shares[i][:, b : b + 1] * ref[b].astype(f32) for i, ref in enumerate(refs)]
-    return functools.reduce(jnp.add, attended)
+    shares = [share / total for share in shares]
+    queries = (parts[0].shape[0] - ROWS) // ROWS
+    eye = lane_index(queries) == row_index(queries)
+    blocks = []
+    for b in range(ROWS):
+        block = None
+        for part, share in zip(parts, shares):
+            column = jnp.sum(jnp.where(eye, share[b : b + 1], 0.0), axis=1, keepdims=True)
+            term = column * part[b * queries : (b + 1) * queries]
+            block = term if block is None else block + term
+        blocks.append(block)
+    return blocks, top + jnp.log(total)
 
 
 def combine_kernel(*refs):
-    refs, out_ref = refs[:-1], refs[-1]
-    shares, logs = shares_of(refs)
-    for b in range(ROWS):
-        out_ref[b] = combined_row(refs, shares, b).astype(bf16)
-    out_ref[ROWS] = pack_logs(logs).astype(bf16)
+    blocks, logs = combined(refs[:-1])
+    refs[-1][...] = jnp.concatenate(blocks + [pack_logs(logs)], axis=0).astype(bf16)
 
 
 def finish_kernel(own_ref, one_ref, two_ref, three_ref, weight_ref, out_ref, attended):
-    refs = (own_ref, one_ref, two_ref, three_ref)
-    shares, _ = shares_of(refs)
-    for b in range(ROWS):
-        queries = shares[0].shape[0]
-        attended[b * queries : (b + 1) * queries, :] = combined_row(refs, shares, b)
+    blocks, _ = combined((own_ref, one_ref, two_ref, three_ref))
+    queries = blocks[0].shape[0]
+    attended[...] = jnp.concatenate(blocks, axis=0)
     heads = queries // STEPS
     rows = jnp.concatenate(
         [
@@ -477,7 +478,7 @@
         [
             ((ALL_ROWS, HEAD), bf16),
             ((ALL_ROWS, HEAD), bf16),
-            ((ROWS + 1, queries, HEAD), bf16),
+            ((ROWS * queries + ROWS, HEAD), bf16),
         ],
         first,
         lengths,

time: 126 us -> 126 us (level)
  no operation moved by 1% of the time
where the time goes in v3:
time: 126 us; the launch traced here: 125 us
  starting transfers between devices  40.4 us (32%)
  blocking collectives  37.7 us (30%)
  waiting for transfers between devices  32.2 us (26%)
  Pallas kernels  8.58 us (7%)
  local copies, waits for them, and re-layouts  4.89 us (4%)
    ppermute x21, starting transfers between devices, from_partners(): lax.ppermute(part, axis, [(i, i ^ flip) for i in range(4)])  37.7 us
    all_to_all x2, blocking collectives, exchange(): return lax.all_to_all(parts, axis, 0, 0, tiled=True)  37.7 us
    ppermute x21, waiting for transfers between devices, from_partners(): lax.ppermute(part, axis, [(i, i ^ flip) for i in range(4)])  22.6 us
    ppermute x5, waiting for transfers between devices, from_other(): return lax.ppermute(part, axis, [(0, 1), (1, 0)])  9.54 us
    pallas_call x11, Pallas kernels, call(): pl.pallas_call(kernel, out_shape=[jax.ShapeDtypeStruct(shape, dtype) for...  8.58 us
    ppermute x5, starting transfers between devices, from_other(): return lax.ppermute(part, axis, [(0, 1), (1, 0)])  2.66 us
  transfers between devices with their start and end apart: 26, of which 18 were waited for; matrix products, arithmetic and copies ran while one was open for 4% of the time, Pallas kernels for 0%

profile of v3, /device:TPU:6, one launch (start us, length us, event | category | flops | bytes accessed | tf_op | source)
XLA Modules:
  0.0 125.4 jit_solution(14292945512623708446)
XLA Ops:
  0.6 2.6 %shard_map.281 = bf16[2,16,32,128]{3,2,1,0:T(8,128)(2,1)} custom-call(bf16[24,256]{1,0:T(8,128)(2,1)} %bitcast.33, f32[1,256]{1,0:T(1,128)} %bitcast.46, bf16[256,2048]{1,0:T(8,128)(2,1)} %wx_hbm.1, bf16[256,2048]{1,0:T(8,128)(2,1)} %wz_hbm.1), custom_call_target="tpu_custom_call" | custom-call | flops 3000000000 | bytes 8388608 | tf_op jit(solution)/shard_map/pallas_call | solution.py:47
  3.2 22.8 %all_to_all.10.in_ref = bf16[32,32,128]{2,1,0:T(8,128)(2,1)S(1)} all-to-all(bf16[32,32,128]{2,1,0:T(8,128)(2,1)} %bitcast.45), channel_id=1, replica_groups=mesh['za'=4,'zb'=2,'x'=4,'y'=4,'core'=2] {'za','zb','x'}, dimensions={0} | all-to-all | bytes 524288 | tf_op jit(solution)/shard_map/all_to_all | solution.py:28
  26.2 14.9 %all_to_all.11.inner_ref.gate_ref = bf16[32,24,128]{2,1,0:T(8,128)(2,1)S(1)} all-to-all(bf16[32,24,128]{2,1,0:T(8,128)(2,1)S(1)} %shard_map.282), channel_id=1, replica_groups=mesh['za'=4,'zb'=2,'x'=4,'y'=4,'core'=2] {'za','zb','x'}, dimensions={0} | all-to-all | bytes 393216 | tf_op jit(solution)/shard_map/all_to_all | solution.py:28
  43.8 1.7 %collective-permute-start.1 = (bf16[24,544]{1,0:T(8,128)(2,1)S(1)}, bf16[24,544]{1,0:T(8,128)(2,1)S(1)}, u32[]{:S(2)}, u32[]{:S(2)}) collective-permute-start(bf16[24,544]{1,0:T(8,128)(2,1)S(1)} %add.27.own_ref), channel_id=1, source_target_pairs={{0,2},{2,0},{4,6},{6,4},{1,3},{3,1},{5,7},{7,5},{8,10},{10,8},{12,... | collective-permute-start | bytes 78344 | tf_op jit(solution)/shard_map/ppermute | solution.py:33
  45.5 2.9 %collective-permute-start.2 = (bf16[24,544]{1,0:T(8,128)(2,1)S(1)}, bf16[24,544]{1,0:T(8,128)(2,1)S(1)}, u32[]{:S(2)}, u32[]{:S(2)}) collective-permute-start(bf16[24,544]{1,0:T(8,128)(2,1)S(1)} %add.27.own_ref), channel_id=1, source_target_pairs={{0,4},{2,6},{4,0},{6,2},{1,5},{3,7},{5,1},{7,3},{8,12},{10,14},{12... | collective-permute-start | bytes 78344 | tf_op jit(solution)/shard_map/ppermute | solution.py:33
  49.5 1.5 %collective-permute-done.2.two_ref = bf16[24,544]{1,0:T(8,128)(2,1)S(1)} collective-permute-done((bf16[24,544]{1,0:T(8,128)(2,1)S(1)}, bf16[24,544]{1,0:T(8,128)(2,1)S(1)}, u32[]{:S(2)}, u32[]{:S(2)}) %collective-permute-start.2) | collective-permute-done | bytes 26144 | tf_op jit(solution)/shard_map/ppermute | solution.py:33
  50.9 2.6 %collective-permute-done.3.three_ref = bf16[24,544]{1,0:T(8,128)(2,1)S(1)} collective-permute-done((bf16[24,544]{1,0:T(8,128)(2,1)S(1)}, bf16[24,544]{1,0:T(8,128)(2,1)S(1)}, u32[]{:S(2)}, u32[]{:S(2)}) %collective-permute-start.3) | collective-permute-done | bytes 26144 | tf_op jit(solution)/shard_map/ppermute | solution.py:33
  53.6 1.6 %shard_map.284 = (f32[16,16,8,128]{3,2,1,0:T(8,128)S(1)}, bf16[24,256]{1,0:T(8,128)(2,1)S(1)}) custom-call(bf16[24,544]{1,0:T(8,128)(2,1)S(1)} %add.27.own_ref, bf16[24,544]{1,0:T(8,128)(2,1)S(1)} %collective-permute-done.1.one_ref, bf16[24,544]{1,0:T(8,128)(2,1)S(1)} %collective-permute-done.2.two_ref, ...), custom_call_target="tpu_custom_call" | custom-call | flops 3000000000 | bytes 8388608 | tf_op jit(solution)/shard_map/pallas_call | solution.py:47
  56.4 1.7 %collective-permute-start.6 = (bf16[24,256]{1,0:T(8,128)(2,1)S(1)}, bf16[24,256]{1,0:T(8,128)(2,1)S(1)}, u32[]{:S(2)}, u32[]{:S(2)}) collective-permute-start(bf16[24,256]{1,0:T(8,128)(2,1)S(1)} %add.28.own_ref), channel_id=1, source_target_pairs={{0,4},{2,6},{4,0},{6,2},{1,5},{3,7},{5,1},{7,3},{8,12},{10,14},{12... | collective-permute-start | bytes 36872 | tf_op jit(solution)/shard_map/ppermute | solution.py:33
  58.1 3.0 %collective-permute-start.7 = (bf16[24,256]{1,0:T(8,128)(2,1)S(1)}, bf16[24,256]{1,0:T(8,128)(2,1)S(1)}, u32[]{:S(2)}, u32[]{:S(2)}) collective-permute-start(bf16[24,256]{1,0:T(8,128)(2,1)S(1)} %add.28.own_ref), channel_id=1, source_target_pairs={{0,6},{2,4},{4,2},{6,0},{1,7},{3,5},{5,3},{7,1},{8,14},{10,12},{12... | collective-permute-start | bytes 36872 | tf_op jit(solution)/shard_map/ppermute | solution.py:33
  63.2 2.1 %collective-permute-start.10 = (bf16[248,128]{1,0:T(8,128)(2,1)S(1)}, bf16[248,128]{1,0:T(8,128)(2,1)S(1)}, u32[]{:S(2)}, u32[]{:S(2)}) collective-permute-start(bf16[248,128]{1,0:T(8,128)(2,1)S(1)} %get-tuple-element.23.refs_0_), channel_id=1, source_target_pairs={{0,24},{8,16},{16,8},{24,0},{1,25},{9,17},{17,9},{25,1},{2,26},{10... | collective-permute-start | bytes 190472 | tf_op jit(solution)/shard_map/ppermute | solution.py:33
  65.4 2.6 %collective-permute-start.9 = (bf16[248,128]{1,0:T(8,128)(2,1)S(1)}, bf16[248,128]{1,0:T(8,128)(2,1)S(1)}, u32[]{:S(2)}, u32[]{:S(2)}) collective-permute-start(bf16[248,128]{1,0:T(8,128)(2,1)S(1)} %get-tuple-element.23.refs_0_), channel_id=1, source_target_pairs={{0,16},{8,24},{16,0},{24,8},{1,17},{9,25},{17,1},{25,9},{2,18},{10... | collective-permute-start | bytes 190472 | tf_op jit(solution)/shard_map/ppermute | solution.py:33
  68.0 1.4 %collective-permute-done.10.refs_3_ = bf16[248,128]{1,0:T(8,128)(2,1)S(1)} collective-permute-done((bf16[248,128]{1,0:T(8,128)(2,1)S(1)}, bf16[248,128]{1,0:T(8,128)(2,1)S(1)}, u32[]{:S(2)}, u32[]{:S(2)}) %collective-permute-start.10) | collective-permute-done | bytes 63520 | tf_op jit(solution)/shard_map/ppermute | solution.py:33
  69.6 1.5 %collective-permute-done.9.refs_2_ = bf16[248,128]{1,0:T(8,128)(2,1)S(1)} collective-permute-done((bf16[248,128]{1,0:T(8,128)(2,1)S(1)}, bf16[248,128]{1,0:T(8,128)(2,1)S(1)}, u32[]{:S(2)}, u32[]{:S(2)}) %collective-permute-start.9) | collective-permute-done | bytes 63520 | tf_op jit(solution)/shard_map/ppermute | solution.py:33
  71.9 3.6 %collective-permute-done.11.refs_1_ = bf16[248,128]{1,0:T(8,128)(2,1)S(1)} collective-permute-done((bf16[248,128]{1,0:T(8,128)(2,1)S(1)}, bf16[248,128]{1,0:T(8,128)(2,1)S(1)}, u32[]{:S(2)}, u32[]{:S(2)}) %collective-permute-start.11) | collective-permute-done | bytes 63520 | tf_op jit(solution)/shard_map/ppermute | solution.py:39
  76.7 2.3 %collective-permute-start.13 = (bf16[248,128]{1,0:T(8,128)(2,1)S(1)}, bf16[248,128]{1,0:T(8,128)(2,1)S(1)}, u32[]{:S(2)}, u32[]{:S(2)}) collective-permute-start(bf16[248,128]{1,0:T(8,128)(2,1)S(1)} %shard_map.287.own_ref), channel_id=1, source_target_pairs={{0,128},{64,192},{128,0},{192,64},{1,129},{65,193},{129,1},{193,65... | collective-permute-start | bytes 190472 | tf_op jit(solution)/shard_map/ppermute | solution.py:33
  79.0 3.2 %collective-permute-start.14 = (bf16[248,128]{1,0:T(8,128)(2,1)S(1)}, bf16[248,128]{1,0:T(8,128)(2,1)S(1)}, u32[]{:S(2)}, u32[]{:S(2)}) collective-permute-start(bf16[248,128]{1,0:T(8,128)(2,1)S(1)} %shard_map.287.own_ref), channel_id=1, source_target_pairs={{0,192},{64,128},{128,64},{192,0},{1,193},{65,129},{129,65},{193,1... | collective-permute-start | bytes 190472 | tf_op jit(solution)/shard_map/ppermute | solution.py:33
  82.2 1.6 %copy.32 = f32[8,16,16,128]{3,2,1,0:T(8,128)} copy(f32[8,16,16,128]{3,0,1,2:T(8,128)S(1)} %bitcast.29) | data formatting | bytes 2097152 | tf_op jit(solution)/shard_map/transpose | solution.py:454
  83.8 2.4 %reshape.73 = f32[8,16,2048]{2,1,0:T(8,128)} reshape(f32[8,16,16,128]{3,2,1,0:T(8,128)} %copy.32) | data formatting | bytes 2097152 | tf_op jit(solution)/shard_map/reshape | solution.py:454
  86.2 1.8 %shard_map.288 = (bf16[24,128]{1,0:T(8,128)(2,1)}, bf16[24,128]{1,0:T(8,128)(2,1)}, bf16[200,128]{1,0:T(8,128)(2,1)S(1)}) custom-call(s32[1]{0:T(128)} %bitcast.13.first_ref, s32[8]{0:T(128)S(1)} %copy-done.21, s32[4,8]{1,0:T(4,128)S(1)} %bitcast.39, bf16[248,128]{1,0:T(8,128)(2,1)S(1)} %shard_map.287.own_ref, ...), custom_call_target="tpu_custom_call" | custom-call | flops 3000000000 | bytes 8388608 | tf_op jit(solution)/shard_map/pallas_call | solution.py:47
  87.9 2.5 %collective-permute-start.15 = (bf16[200,128]{1,0:T(8,128)(2,1)S(1)}, bf16[200,128]{1,0:T(8,128)(2,1)S(1)}, u32[]{:S(2)}, u32[]{:S(2)}) collective-permute-start(bf16[200,128]{1,0:T(8,128)(2,1)S(1)} %get-tuple-element.28.refs_0_), channel_id=1, source_target_pairs={{0,8},{8,0},{16,24},{24,16},{1,9},{9,1},{17,25},{25,17},{2,10},{10... | collective-permute-start | bytes 153608 | tf_op jit(solution)/shard_map/ppermute | solution.py:33
  91.2 1.9 %collective-permute-start.17 = (bf16[200,128]{1,0:T(8,128)(2,1)S(1)}, bf16[200,128]{1,0:T(8,128)(2,1)S(1)}, u32[]{:S(2)}, u32[]{:S(2)}) collective-permute-start(bf16[200,128]{1,0:T(8,128)(2,1)S(1)} %get-tuple-element.28.refs_0_), channel_id=1, source_target_pairs={{0,24},{8,16},{16,8},{24,0},{1,25},{9,17},{17,9},{25,1},{2,26},{10... | collective-permute-start | bytes 153608 | tf_op jit(solution)/shard_map/ppermute | solution.py:33
  93.1 2.9 %collective-permute-done.16.refs_2_ = bf16[200,128]{1,0:T(8,128)(2,1)S(1)} collective-permute-done((bf16[200,128]{1,0:T(8,128)(2,1)S(1)}, bf16[200,128]{1,0:T(8,128)(2,1)S(1)}, u32[]{:S(2)}, u32[]{:S(2)}) %collective-permute-start.16) | collective-permute-done | bytes 51232 | tf_op jit(solution)/shard_map/ppermute | solution.py:33
  96.9 1.8 %collective-permute-start.18 = (bf16[200,128]{1,0:T(8,128)(2,1)S(1)}, bf16[200,128]{1,0:T(8,128)(2,1)S(1)}, u32[]{:S(2)}, u32[]{:S(2)}) collective-permute-start(bf16[200,128]{1,0:T(8,128)(2,1)S(1)} %shard_map.289.refs_0_), channel_id=1, source_target_pairs={{0,32},{32,0},{1,33},{33,1},{2,34},{34,2},{3,35},{35,3},{4,36},{36... | collective-permute-start | bytes 153608 | tf_op jit(solution)/shard_map/ppermute | solution.py:39
  98.7 2.4 %collective-permute-done.18.refs_1_ = bf16[200,128]{1,0:T(8,128)(2,1)S(1)} collective-permute-done((bf16[200,128]{1,0:T(8,128)(2,1)S(1)}, bf16[200,128]{1,0:T(8,128)(2,1)S(1)}, u32[]{:S(2)}, u32[]{:S(2)}) %collective-permute-start.18) | collective-permute-done | bytes 51232 | tf_op jit(solution)/shard_map/ppermute | solution.py:39
  101.3 1.8 %collective-permute-start.19 = (bf16[200,128]{1,0:T(8,128)(2,1)S(1)}, bf16[200,128]{1,0:T(8,128)(2,1)S(1)}, u32[]{:S(2)}, u32[]{:S(2)}) collective-permute-start(bf16[200,128]{1,0:T(8,128)(2,1)S(1)} %shard_map.290.own_ref), channel_id=1, source_target_pairs={{0,64},{64,0},{128,192},{192,128},{1,65},{65,1},{129,193},{193,129... | collective-permute-start | bytes 153608 | tf_op jit(solution)/shard_map/ppermute | solution.py:33
  103.1 3.7 %collective-permute-start.20 = (bf16[200,128]{1,0:T(8,128)(2,1)S(1)}, bf16[200,128]{1,0:T(8,128)(2,1)S(1)}, u32[]{:S(2)}, u32[]{:S(2)}) collective-permute-start(bf16[200,128]{1,0:T(8,128)(2,1)S(1)} %shard_map.290.own_ref), channel_id=1, source_target_pairs={{0,128},{64,192},{128,0},{192,64},{1,129},{65,193},{129,1},{193,65... | collective-permute-start | bytes 153608 | tf_op jit(solution)/shard_map/ppermute | solution.py:33
  107.9 3.3 %collective-permute-done.20.two_ref = bf16[200,128]{1,0:T(8,128)(2,1)S(1)} collective-permute-done((bf16[200,128]{1,0:T(8,128)(2,1)S(1)}, bf16[200,128]{1,0:T(8,128)(2,1)S(1)}, u32[]{:S(2)}, u32[]{:S(2)}) %collective-permute-start.20) | collective-permute-done | bytes 51232 | tf_op jit(solution)/shard_map/ppermute | solution.py:33
  111.2 1.9 %collective-permute-done.21.three_ref = bf16[200,128]{1,0:T(8,128)(2,1)S(1)} collective-permute-done((bf16[200,128]{1,0:T(8,128)(2,1)S(1)}, bf16[200,128]{1,0:T(8,128)(2,1)S(1)}, u32[]{:S(2)}, u32[]{:S(2)}) %collective-permute-start.21) | collective-permute-done | bytes 51232 | tf_op jit(solution)/shard_map/ppermute | solution.py:33
  115.5 4.4 %collective-permute-start.24 = (bf16[24,256]{1,0:T(8,128)(2,1)S(1)}, bf16[24,256]{1,0:T(8,128)(2,1)S(1)}, u32[]{:S(2)}, u32[]{:S(2)}) collective-permute-start(bf16[24,256]{1,0:T(8,128)(2,1)S(1)} %add.31), channel_id=1, source_target_pairs={{0,4},{2,6},{4,0},{6,2},{1,5},{3,7},{5,1},{7,3},{8,12},{10,14},{12... | collective-permute-start | bytes 36872 | tf_op jit(solution)/shard_map/ppermute | solution.py:33
  119.8 1.8 %collective-permute-done.24 = bf16[24,256]{1,0:T(8,128)(2,1)S(1)} collective-permute-done((bf16[24,256]{1,0:T(8,128)(2,1)S(1)}, bf16[24,256]{1,0:T(8,128)(2,1)S(1)}, u32[]{:S(2)}, u32[]{:S(2)}) %collective-permute-start.24) | collective-permute-done | bytes 12320 | tf_op jit(solution)/shard_map/ppermute | solution.py:33
  121.6 3.1 %collective-permute-done.25 = bf16[24,256]{1,0:T(8,128)(2,1)S(1)} collective-permute-done((bf16[24,256]{1,0:T(8,128)(2,1)S(1)}, bf16[24,256]{1,0:T(8,128)(2,1)S(1)}, u32[]{:S(2)}, u32[]{:S(2)}) %collective-permute-start.25) | collective-permute-done | bytes 12320 | tf_op jit(solution)/shard_map/ppermute | solution.py:33
  (87 shorter events, 15.3 us)
Async XLA Ops:
  26.0 15.1 %copy-start = (bf16[2048,544]{0,1:T(8,128)(2,1)S(1)}, bf16[2048,544]{0,1:T(8,128)(2,1)}, u32[]{:S(2)}) copy-start(bf16[2048,544]{0,1:T(8,128)(2,1)} %param.32) | copy-start | bytes 6684676
  26.0 15.1 %copy-start.7 = (f32[8,3,2048]{2,0,1:T(8,128)S(1)}, f32[8,3,2048]{2,0,1:T(8,128)}, u32[]{:S(2)}) copy-start(f32[8,3,2048]{2,0,1:T(8,128)} %param.50) | copy-start | bytes 589828
  26.0 15.1 %copy-start.11 = (f32[4,2048]{1,0:T(4,128)S(1)}, f32[4,2048]{1,0:T(4,128)}, u32[]{:S(2)}) copy-start(f32[4,2048]{1,0:T(4,128)} %taps_ref.1) | copy-start | bytes 98308
  26.0 15.1 %copy-start.13 = (f32[2048]{0:T(1024)S(1)}, f32[2048]{0:T(1024)}, u32[]{:S(2)}) copy-start(f32[2048]{0:T(1024)} %param.31) | copy-start | bytes 24580
  42.5 11.0 %copy-start.15 = (f32[2048]{0:T(1024)S(1)}, f32[2048]{0:T(1024)}, u32[]{:S(2)}) copy-start(f32[2048]{0:T(1024)} %param.39) | copy-start | bytes 24580
  42.5 1.3 %collective-permute-start = (bf16[24,544]{1,0:T(8,128)(2,1)S(1)}, bf16[24,544]{1,0:T(8,128)(2,1)S(1)}, u32[]{:S(2)}, u32[]{:S(2)}) collective-permute-start(bf16[24,544]{1,0:T(8,128)(2,1)S(1)} %get-tuple-element.19), channel_id=1, source_target_pairs={{0,1},{1,0},{2,3},{3,2},{4,5},{5,4},{6,7},{7,6},{8,9},{9,8},{10,11... | collective-permute-start | bytes 78344 | tf_op jit(solution)/shard_map/ppermute | solution.py:39
  43.8 5.6 %collective-permute-start.1 = (bf16[24,544]{1,0:T(8,128)(2,1)S(1)}, bf16[24,544]{1,0:T(8,128)(2,1)S(1)}, u32[]{:S(2)}, u32[]{:S(2)}) collective-permute-start(bf16[24,544]{1,0:T(8,128)(2,1)S(1)} %add.27.own_ref), channel_id=1, source_target_pairs={{0,2},{2,0},{4,6},{6,4},{1,3},{3,1},{5,7},{7,5},{8,10},{10,8},{12,... | collective-permute-start | bytes 78344 | tf_op jit(solution)/shard_map/ppermute | solution.py:33
  45.5 5.4 %collective-permute-start.2 = (bf16[24,544]{1,0:T(8,128)(2,1)S(1)}, bf16[24,544]{1,0:T(8,128)(2,1)S(1)}, u32[]{:S(2)}, u32[]{:S(2)}) collective-permute-start(bf16[24,544]{1,0:T(8,128)(2,1)S(1)} %add.27.own_ref), channel_id=1, source_target_pairs={{0,4},{2,6},{4,0},{6,2},{1,5},{3,7},{5,1},{7,3},{8,12},{10,14},{12... | collective-permute-start | bytes 78344 | tf_op jit(solution)/shard_map/ppermute | solution.py:33
  48.4 5.1 %collective-permute-start.3 = (bf16[24,544]{1,0:T(8,128)(2,1)S(1)}, bf16[24,544]{1,0:T(8,128)(2,1)S(1)}, u32[]{:S(2)}, u32[]{:S(2)}) collective-permute-start(bf16[24,544]{1,0:T(8,128)(2,1)S(1)} %add.27.own_ref), channel_id=1, source_target_pairs={{0,6},{2,4},{4,2},{6,0},{1,7},{3,5},{5,3},{7,1},{8,14},{10,12},{12... | collective-permute-start | bytes 78344 | tf_op jit(solution)/shard_map/ppermute | solution.py:33
  55.2 1.2 collective-permute-start.4
  56.4 4.7 %collective-permute-start.5 = (bf16[24,256]{1,0:T(8,128)(2,1)S(1)}, bf16[24,256]{1,0:T(8,128)(2,1)S(1)}, u32[]{:S(2)}, u32[]{:S(2)}) collective-permute-start(bf16[24,256]{1,0:T(8,128)(2,1)S(1)} %add.28.own_ref), channel_id=1, source_target_pairs={{0,2},{2,0},{4,6},{6,4},{1,3},{3,1},{5,7},{7,5},{8,10},{10,8},{12,... | collective-permute-start | bytes 36872 | tf_op jit(solution)/shard_map/ppermute | solution.py:33
  56.4 5.4 %collective-permute-start.6 = (bf16[24,256]{1,0:T(8,128)(2,1)S(1)}, bf16[24,256]{1,0:T(8,128)(2,1)S(1)}, u32[]{:S(2)}, u32[]{:S(2)}) collective-permute-start(bf16[24,256]{1,0:T(8,128)(2,1)S(1)} %add.28.own_ref), channel_id=1, source_target_pairs={{0,4},{2,6},{4,0},{6,2},{1,5},{3,7},{5,1},{7,3},{8,12},{10,14},{12... | collective-permute-start | bytes 36872 | tf_op jit(solution)/shard_map/ppermute | solution.py:33
  58.1 4.9 %collective-permute-start.7 = (bf16[24,256]{1,0:T(8,128)(2,1)S(1)}, bf16[24,256]{1,0:T(8,128)(2,1)S(1)}, u32[]{:S(2)}, u32[]{:S(2)}) collective-permute-start(bf16[24,256]{1,0:T(8,128)(2,1)S(1)} %add.28.own_ref), channel_id=1, source_target_pairs={{0,6},{2,4},{4,2},{6,0},{1,7},{3,5},{5,3},{7,1},{8,14},{10,12},{12... | collective-permute-start | bytes 36872 | tf_op jit(solution)/shard_map/ppermute | solution.py:33
  63.2 6.1 %collective-permute-start.10 = (bf16[248,128]{1,0:T(8,128)(2,1)S(1)}, bf16[248,128]{1,0:T(8,128)(2,1)S(1)}, u32[]{:S(2)}, u32[]{:S(2)}) collective-permute-start(bf16[248,128]{1,0:T(8,128)(2,1)S(1)} %get-tuple-element.23.refs_0_), channel_id=1, source_target_pairs={{0,24},{8,16},{16,8},{24,0},{1,25},{9,17},{17,9},{25,1},{2,26},{10... | collective-permute-start | bytes 190472 | tf_op jit(solution)/shard_map/ppermute | solution.py:33
  65.4 4.2 %collective-permute-start.8 = (bf16[248,128]{1,0:T(8,128)(2,1)S(1)}, bf16[248,128]{1,0:T(8,128)(2,1)S(1)}, u32[]{:S(2)}, u32[]{:S(2)}) collective-permute-start(bf16[248,128]{1,0:T(8,128)(2,1)S(1)} %get-tuple-element.23.refs_0_), channel_id=1, source_target_pairs={{0,8},{8,0},{16,24},{24,16},{1,9},{9,1},{17,25},{25,17},{2,10},{10... | collective-permute-start | bytes 190472 | tf_op jit(solution)/shard_map/ppermute | solution.py:33
  65.4 5.7 %collective-permute-start.9 = (bf16[248,128]{1,0:T(8,128)(2,1)S(1)}, bf16[248,128]{1,0:T(8,128)(2,1)S(1)}, u32[]{:S(2)}, u32[]{:S(2)}) collective-permute-start(bf16[248,128]{1,0:T(8,128)(2,1)S(1)} %get-tuple-element.23.refs_0_), channel_id=1, source_target_pairs={{0,16},{8,24},{16,0},{24,8},{1,17},{9,25},{17,1},{25,9},{2,18},{10... | collective-permute-start | bytes 190472 | tf_op jit(solution)/shard_map/ppermute | solution.py:33
  71.2 4.3 %collective-permute-start.11 = (bf16[248,128]{1,0:T(8,128)(2,1)S(1)}, bf16[248,128]{1,0:T(8,128)(2,1)S(1)}, u32[]{:S(2)}, u32[]{:S(2)}) collective-permute-start(bf16[248,128]{1,0:T(8,128)(2,1)S(1)} %shard_map.286.refs_0_), channel_id=1, source_target_pairs={{0,32},{32,0},{1,33},{33,1},{2,34},{34,2},{3,35},{35,3},{4,36},{36... | collective-permute-start | bytes 190472 | tf_op jit(solution)/shard_map/ppermute | solution.py:39
  75.6 10.6 %collective-permute-start.12 = (bf16[248,128]{1,0:T(8,128)(2,1)S(1)}, bf16[248,128]{1,0:T(8,128)(2,1)S(1)}, u32[]{:S(2)}, u32[]{:S(2)}) collective-permute-start(bf16[248,128]{1,0:T(8,128)(2,1)S(1)} %shard_map.287.own_ref), channel_id=1, source_target_pairs={{0,64},{64,0},{128,192},{192,128},{1,65},{65,1},{129,193},{193,129... | collective-permute-start | bytes 190472 | tf_op jit(solution)/shard_map/ppermute | solution.py:33
  76.7 9.5 %collective-permute-start.13 = (bf16[248,128]{1,0:T(8,128)(2,1)S(1)}, bf16[248,128]{1,0:T(8,128)(2,1)S(1)}, u32[]{:S(2)}, u32[]{:S(2)}) collective-permute-start(bf16[248,128]{1,0:T(8,128)(2,1)S(1)} %shard_map.287.own_ref), channel_id=1, source_target_pairs={{0,128},{64,192},{128,0},{192,64},{1,129},{65,193},{129,1},{193,65... | collective-permute-start | bytes 190472 | tf_op jit(solution)/shard_map/ppermute | solution.py:33
  79.0 7.2 %collective-permute-start.14 = (bf16[248,128]{1,0:T(8,128)(2,1)S(1)}, bf16[248,128]{1,0:T(8,128)(2,1)S(1)}, u32[]{:S(2)}, u32[]{:S(2)}) collective-permute-start(bf16[248,128]{1,0:T(8,128)(2,1)S(1)} %shard_map.287.own_ref), channel_id=1, source_target_pairs={{0,192},{64,128},{128,64},{192,0},{1,193},{65,129},{129,65},{193,1... | collective-permute-start | bytes 190472 | tf_op jit(solution)/shard_map/ppermute | solution.py:33
  87.9 5.2 %collective-permute-start.15 = (bf16[200,128]{1,0:T(8,128)(2,1)S(1)}, bf16[200,128]{1,0:T(8,128)(2,1)S(1)}, u32[]{:S(2)}, u32[]{:S(2)}) collective-permute-start(bf16[200,128]{1,0:T(8,128)(2,1)S(1)} %get-tuple-element.28.refs_0_), channel_id=1, source_target_pairs={{0,8},{8,0},{16,24},{24,16},{1,9},{9,1},{17,25},{25,17},{2,10},{10... | collective-permute-start | bytes 153608 | tf_op jit(solution)/shard_map/ppermute | solution.py:33
  90.4 5.6 %collective-permute-start.16 = (bf16[200,128]{1,0:T(8,128)(2,1)S(1)}, bf16[200,128]{1,0:T(8,128)(2,1)S(1)}, u32[]{:S(2)}, u32[]{:S(2)}) collective-permute-start(bf16[200,128]{1,0:T(8,128)(2,1)S(1)} %get-tuple-element.28.refs_0_), channel_id=1, source_target_pairs={{0,16},{8,24},{16,0},{24,8},{1,17},{9,25},{17,1},{25,9},{2,18},{10... | collective-permute-start | bytes 153608 | tf_op jit(solution)/shard_map/ppermute | solution.py:33
  91.2 5.3 %collective-permute-start.17 = (bf16[200,128]{1,0:T(8,128)(2,1)S(1)}, bf16[200,128]{1,0:T(8,128)(2,1)S(1)}, u32[]{:S(2)}, u32[]{:S(2)}) collective-permute-start(bf16[200,128]{1,0:T(8,128)(2,1)S(1)} %get-tuple-element.28.refs_0_), channel_id=1, source_target_pairs={{0,24},{8,16},{16,8},{24,0},{1,25},{9,17},{17,9},{25,1},{2,26},{10... | collective-permute-start | bytes 153608 | tf_op jit(solution)/shard_map/ppermute | solution.py:33
  96.9 16.2 %copy-start.6 = (bf16[1024,256]{1,0:T(8,128)(2,1)S(1)}, bf16[1024,256]{1,0:T(8,128)(2,1)}, u32[]{:S(2)}) copy-start(bf16[1024,256]{1,0:T(8,128)(2,1)} %weight_ref.1) | copy-start | bytes 1572868
  96.9 4.2 %collective-permute-start.18 = (bf16[200,128]{1,0:T(8,128)(2,1)S(1)}, bf16[200,128]{1,0:T(8,128)(2,1)S(1)}, u32[]{:S(2)}, u32[]{:S(2)}) collective-permute-start(bf16[200,128]{1,0:T(8,128)(2,1)S(1)} %shard_map.289.refs_0_), channel_id=1, source_target_pairs={{0,32},{32,0},{1,33},{33,1},{2,34},{34,2},{3,35},{35,3},{4,36},{36... | collective-permute-start | bytes 153608 | tf_op jit(solution)/shard_map/ppermute | solution.py:39
  101.3 6.6 %collective-permute-start.19 = (bf16[200,128]{1,0:T(8,128)(2,1)S(1)}, bf16[200,128]{1,0:T(8,128)(2,1)S(1)}, u32[]{:S(2)}, u32[]{:S(2)}) collective-permute-start(bf16[200,128]{1,0:T(8,128)(2,1)S(1)} %shard_map.290.own_ref), channel_id=1, source_target_pairs={{0,64},{64,0},{128,192},{192,128},{1,65},{65,1},{129,193},{193,129... | collective-permute-start | bytes 153608 | tf_op jit(solution)/shard_map/ppermute | solution.py:33
  103.1 8.0 %collective-permute-start.20 = (bf16[200,128]{1,0:T(8,128)(2,1)S(1)}, bf16[200,128]{1,0:T(8,128)(2,1)S(1)}, u32[]{:S(2)}, u32[]{:S(2)}) collective-permute-start(bf16[200,128]{1,0:T(8,128)(2,1)S(1)} %shard_map.290.own_ref), channel_id=1, source_target_pairs={{0,128},{64,192},{128,0},{192,64},{1,129},{65,193},{129,1},{193,65... | collective-permute-start | bytes 153608 | tf_op jit(solution)/shard_map/ppermute | solution.py:33
  106.9 6.2 %collective-permute-start.21 = (bf16[200,128]{1,0:T(8,128)(2,1)S(1)}, bf16[200,128]{1,0:T(8,128)(2,1)S(1)}, u32[]{:S(2)}, u32[]{:S(2)}) collective-permute-start(bf16[200,128]{1,0:T(8,128)(2,1)S(1)} %shard_map.290.own_ref), channel_id=1, source_target_pairs={{0,192},{64,128},{128,64},{192,0},{1,193},{65,129},{129,65},{193,1... | collective-permute-start | bytes 153608 | tf_op jit(solution)/shard_map/ppermute | solution.py:33
  113.5 1.2 collective-permute-start.22
  114.7 5.2 %collective-permute-start.23 = (bf16[24,256]{1,0:T(8,128)(2,1)S(1)}, bf16[24,256]{1,0:T(8,128)(2,1)S(1)}, u32[]{:S(2)}, u32[]{:S(2)}) collective-permute-start(bf16[24,256]{1,0:T(8,128)(2,1)S(1)} %add.31), channel_id=1, source_target_pairs={{0,2},{2,0},{4,6},{6,4},{1,3},{3,1},{5,7},{7,5},{8,10},{10,8},{12,... | collective-permute-start | bytes 36872 | tf_op jit(solution)/shard_map/ppermute | solution.py:33
  115.5 6.2 %collective-permute-start.24 = (bf16[24,256]{1,0:T(8,128)(2,1)S(1)}, bf16[24,256]{1,0:T(8,128)(2,1)S(1)}, u32[]{:S(2)}, u32[]{:S(2)}) collective-permute-start(bf16[24,256]{1,0:T(8,128)(2,1)S(1)} %add.31), channel_id=1, source_target_pairs={{0,4},{2,6},{4,0},{6,2},{1,5},{3,7},{5,1},{7,3},{8,12},{10,14},{12... | collective-permute-start | bytes 36872 | tf_op jit(solution)/shard_map/ppermute | solution.py:33
  119.8 4.9 %collective-permute-start.25 = (bf16[24,256]{1,0:T(8,128)(2,1)S(1)}, bf16[24,256]{1,0:T(8,128)(2,1)S(1)}, u32[]{:S(2)}, u32[]{:S(2)}) collective-permute-start(bf16[24,256]{1,0:T(8,128)(2,1)S(1)} %add.31), channel_id=1, source_target_pairs={{0,6},{2,4},{4,2},{6,0},{1,7},{3,5},{5,3},{7,1},{8,14},{10,12},{12... | collective-permute-start | bytes 36872 | tf_op jit(solution)/shard_map/ppermute | solution.py:33
  (17 other events, 174.2 us)
